TPU v7x, 256 devices: a whole 4x4x8 slice. The times are simulated.
256 devices in a mesh: dp: 8 (over x, core), seq: 32 (over y, z).
Axes of the slice: x: 4, y: 4, z: 8, core: 2. Of those that a mesh axis runs over, the one named last changes fastest.
Arguments:
- node_queries: bfloat16 [8, 4096, 1024], P('dp', 'seq'), may hold values from -6 to 6
- node_keys: bfloat16 [8, 4096, 1024], P('dp', 'seq'), may hold values from -6 to 6
- node_values: bfloat16 [8, 4096, 1024], P('dp', 'seq'), may hold values from -6 to 6
- cotangent: bfloat16 [8, 4096, 1024], P('dp', 'seq'), may hold values from -6 to 6
- w_out: bfloat16 [1024, 1024], replicated, may hold values from -0.1875 to 0.1875
- neighbours: int32 [8, 32, 4], P('dp'), may hold values from -1 to 31, as said below
- contacts: int32 [8, 32, 8], P('dp'), may hold values from -1 to 31, as said below
- ownership: int32 [8, 32], P('dp'), may hold values from 0 to 3, never falling along the last dimension, each value on 1 to 16 neighbouring positions
Outputs:
- output: bfloat16 [8, 4096, 1024], P('dp', 'seq')
- query_gradient: bfloat16 [8, 4096, 1024], P('dp', 'seq')
- key_grad: bfloat16 [8, 4096, 1024], P('dp', 'seq')
- value_grad: bfloat16 [8, 4096, 1024], P('dp', 'seq')
- weight_grad: float32 [1024, 1024], P('seq')
Inputs may be any that keep to these rules, and one draw needn't show every extreme that they name: `neighbours`: entry n of block b's row is b + o with o = -2, -1, 1, 2 for n = 0, 1, 2, 3, or -1; it is -1 where b + o lies outside the scene, and in some other slots. `contacts`: in each row the live entries come first and the rest are -1; live entries are distinct blocks that lie more than 2 blocks away from the row's own block. `ownership`: ownership never falls from one block to the next.
All inputs are finite; a program needn't handle non-finite values.
Results may differ from a plain program's by a relative error of at most 0.015.
Values may be sent and summed in bfloat16 or wider, within the bound.
A program may use at most 64 MiB of HBM per device.

v0:
```python
import math

import jax
import jax.numpy as jnp
from jax import lax
from jax.sharding import PartitionSpec as P

HEADS = 16
HDIM = 64
BLK = 128


def block_table(neighbours, contacts, ownership):
    block_count = neighbours.shape[0]
    block_ids = jnp.arange(block_count, dtype=jnp.int32)
    matches = contacts[:, :, None] == block_ids[None, None, :]
    shared = jnp.any(matches & (ownership[None, None, :] == ownership[:, None, None]), axis=-1)
    slot_table = jnp.concatenate([block_ids[:, None], neighbours, contacts], axis=1)
    slot_valid = jnp.concatenate(
        [
            jnp.ones((block_count, 1), dtype=bool),
            neighbours >= 0,
            (contacts >= 0) & jnp.logical_not(shared),
        ],
        axis=1,
    )
    return (jnp.maximum(slot_table, 0), slot_valid)


def scores_for(query_group, selected_key_rows, valid_group):
    logit_scores = (
        jnp.einsum(
            "bqpd,bskpd->bpqsk", query_group, selected_key_rows, preferred_element_type=jnp.float32
        )
        * 0.125
    )
    return jnp.where(valid_group[:, None, None, :, None], logit_scores, -jnp.inf)


def forward_group(query_group, key_blocks, value_blocks, table_group, valid_group):
    selected_key_rows = key_blocks[table_group]
    selected_value_rows = value_blocks[table_group]
    logit_scores = scores_for(query_group, selected_key_rows, valid_group)
    row_max = jnp.max(logit_scores, axis=(3, 4), keepdims=True)
    log_total = row_max + jnp.log(
        jnp.sum(jnp.exp(logit_scores - row_max), axis=(3, 4), keepdims=True)
    )
    softmax_weights = jnp.exp(logit_scores - log_total).astype(jnp.bfloat16)
    mixed_rows = jnp.einsum(
        "bpqsk,bskpd->bqpd",
        softmax_weights,
        selected_value_rows,
        preferred_element_type=jnp.float32,
    )
    return (mixed_rows.astype(jnp.bfloat16), log_total)


def backward_group(
    query_group,
    grad_group,
    mixed_group,
    key_blocks,
    value_blocks,
    table_group,
    valid_group,
    log_total,
):
    selected_key_rows = key_blocks[table_group]
    selected_value_rows = value_blocks[table_group]
    probabilities = jnp.exp(scores_for(query_group, selected_key_rows, valid_group) - log_total)
    softmax_weights = probabilities.astype(jnp.bfloat16)
    row_delta = jnp.einsum(
        "bqpd,bqpd->bpq", grad_group, mixed_group, preferred_element_type=jnp.float32
    )
    probability_gradient = jnp.einsum(
        "bqpd,bskpd->bpqsk", grad_group, selected_value_rows, preferred_element_type=jnp.float32
    )
    score_gradient = (
        probabilities * (probability_gradient - row_delta[:, :, :, None, None])
    ).astype(jnp.bfloat16)
    query_gradient = (
        jnp.einsum(
            "bpqsk,bskpd->bqpd",
            score_gradient,
            selected_key_rows,
            preferred_element_type=jnp.float32,
        )
        * 0.125
    )
    key_products = (
        jnp.einsum(
            "bpqsk,bqpd->bskpd", score_gradient, query_group, preferred_element_type=jnp.float32
        )
        * 0.125
    )
    value_products = jnp.einsum(
        "bpqsk,bqpd->bskpd", softmax_weights, grad_group, preferred_element_type=jnp.float32
    )
    return (query_gradient.astype(jnp.bfloat16), jnp.stack([key_products, value_products], axis=3))


def local(node_queries, node_keys, node_values, cotangent, w_out, neighbours, contacts, ownership):
    seq_size = lax.axis_size("seq")
    node_rows = node_queries.shape[1]
    head_share = max(HEADS // seq_size, 1)
    half_count = max(seq_size // HEADS, 1)
    group_count = HEADS // head_share
    group_width = head_share * HDIM
    block_count = neighbours.shape[1]
    block_rows = BLK // half_count
    batch_blocks = math.gcd(block_count, max(1, 512 // block_rows))
    batch_count = block_count // batch_blocks
    local_rows = node_rows // half_count
    feature_count = w_out.shape[0]
    slot_table, slot_valid = block_table(neighbours[0], contacts[0], ownership[0])
    table_batches = slot_table.reshape(batch_count, batch_blocks, -1)
    valid_batches = slot_valid.reshape(batch_count, batch_blocks, -1)
    grad_out = cotangent[0]
    attention_grad = lax.dot_general(
        grad_out, w_out, (((1,), (1,)), ((), ())), preferred_element_type=jnp.float32
    ).astype(jnp.bfloat16)

    def to_heads(matrix):
        return matrix.reshape(local_rows, seq_size, group_width)

    def to_batches(matrix):
        return matrix.reshape(batch_count, batch_blocks, block_rows, head_share, HDIM)

    query_heads = lax.all_to_all(
        to_heads(node_queries[0]), "seq", split_axis=1, concat_axis=0, tiled=True
    )
    key_value = jnp.concatenate(
        [
            node_keys[0].reshape(node_rows, group_count, group_width),
            node_values[0].reshape(node_rows, group_count, group_width),
        ],
        axis=2,
    )
    key_value = jnp.broadcast_to(
        key_value[:, None], (node_rows, half_count, group_count, 2 * group_width)
    )
    key_value = key_value.reshape(node_rows, seq_size, 2 * group_width)
    gathered = lax.all_to_all(key_value, "seq", split_axis=1, concat_axis=0, tiled=True)
    gathered = gathered.reshape(block_count, BLK, 2, head_share, HDIM)
    key_blocks = gathered[:, :, 0]
    value_blocks = gathered[:, :, 1]
    query_batches = to_batches(query_heads)

    def forward_step(inputs):
        return forward_group(inputs[0], key_blocks, value_blocks, inputs[1], inputs[2])

    mixed_batches, log_totals = lax.map(forward_step, (query_batches, table_batches, valid_batches))
    attention_result = lax.all_to_all(
        mixed_batches.reshape(seq_size, local_rows, 1, group_width),
        "seq",
        split_axis=0,
        concat_axis=2,
        tiled=True,
    )
    attention_result = attention_result.reshape(node_rows, group_count * group_width)
    output = jnp.dot(attention_result, w_out, preferred_element_type=jnp.float32).astype(
        jnp.bfloat16
    )
    grad_heads = lax.all_to_all(
        to_heads(attention_grad), "seq", split_axis=1, concat_axis=0, tiled=True
    )

    def backward_step(running, inputs):
        query_group, grad_group, mixed_group, table_group, valid_group, log_total = inputs
        query_part, terms = backward_group(
            query_group,
            grad_group,
            mixed_group,
            key_blocks,
            value_blocks,
            table_group,
            valid_group,
            log_total,
        )
        return (running.at[table_group].add(terms), query_part)

    start_value = jnp.zeros((block_count, BLK, 2, head_share, HDIM), jnp.float32)
    summed, query_parts = lax.scan(
        backward_step,
        start_value,
        (
            query_batches,
            to_batches(grad_heads),
            mixed_batches,
            table_batches,
            valid_batches,
            log_totals,
        ),
    )
    query_gradient = lax.all_to_all(
        query_parts.reshape(seq_size, local_rows, 1, group_width),
        "seq",
        split_axis=0,
        concat_axis=2,
        tiled=True,
    )
    query_gradient = query_gradient.reshape(node_rows, group_count * group_width)
    returned = lax.all_to_all(
        summed.reshape(seq_size, node_rows, 1, 2 * group_width),
        "seq",
        split_axis=0,
        concat_axis=2,
        tiled=True,
    )
    returned = jnp.sum(returned.reshape(node_rows, half_count, group_count, 2, group_width), axis=1)
    key_grad = returned[:, :, 0].reshape(node_rows, group_count * group_width).astype(jnp.bfloat16)
    value_grad = (
        returned[:, :, 1].reshape(node_rows, group_count * group_width).astype(jnp.bfloat16)
    )
    share_rows = feature_count // seq_size
    grad_scale = (lax.axis_size("dp") * block_count * BLK) ** (-0.5)
    whole = lax.dot_general(
        attention_result, grad_out, (((0,), (0,)), ((), ())), preferred_element_type=jnp.float32
    )
    summed_whole = lax.psum(whole, ("dp", "seq"))
    weight_grad = lax.dynamic_slice_in_dim(
        summed_whole, lax.axis_index("seq") * share_rows, share_rows, 0
    )
    weight_grad = weight_grad * grad_scale
    return (output[None], query_gradient[None], key_grad[None], value_grad[None], weight_grad)


def solution(mesh):
    placed = (
        P("dp", "seq", None),
        P("dp", "seq", None),
        P("dp", "seq", None),
        P("dp", "seq", None),
        P(),
        P("dp", None, None),
        P("dp", None, None),
        P("dp", None),
    )
    return jax.shard_map(
        local,
        mesh=mesh,
        in_specs=placed,
        out_specs=(
            P("dp", "seq", None),
            P("dp", "seq", None),
            P("dp", "seq", None),
            P("dp", "seq", None),
            P("seq", None),
        ),
        check_vma=False,
    )
```

profile of v0, /device:TPU:17, one launch (start us, length us, event | category | flops | bytes accessed | tf_op | source)
XLA Modules:
  0.0 636.2 jit_solution(13721861302718774347)
XLA Ops:
  7.2 1.6 copy-done
  8.8 1.8 convolution_convert_fusion
  12.2 11.0 %all-to-all-start.3 = ((bf16[32,2,2048]{2,1,0:T(2,128)(2,1)}), bf16[32,2,2048]{2,1,0:T(2,128)(2,1)S(1)}, u32[]{:S(2)}, u32[]{:S(2)}) async-start(bf16[32,2,2048]{2,1,0:T(2,128)(2,1)} %reshape.398), calls=%async_computation.3 | async-start | bytes 524288 | tf_op jit(solution)/shard_map/all_to_all | solution.py:164
  25.9 5.6 all-to-all-done.3
  31.6 7.7 %all-to-all-start.1 = ((bf16[32,2,2048]{2,1,0:T(2,128)(2,1)}), bf16[32,2,2048]{2,1,0:T(2,128)(2,1)S(1)}, u32[]{:S(2)}, u32[]{:S(2)}) async-start(bf16[32,2,2048]{2,1,0:T(2,128)(2,1)} %reshape.394), calls=%async_computation.1 | async-start | bytes 524288 | tf_op jit(solution)/shard_map/all_to_all | solution.py:129
  40.4 1.8 copy.88
  43.1 4.4 all-to-all-done.1
  48.8 7.1 %all-to-all-start = ((bf16[128,32,128]{0,2,1:T(8,128)(2,1)}), bf16[128,32,128]{0,2,1:T(8,128)(2,1)S(1)}, u32[]{:S(2)}, u32[]{:S(2)}) async-start(bf16[128,32,128]{0,2,1:T(8,128)(2,1)} %bitcast.288), calls=%async_computation | async-start | bytes 2097152 | tf_op jit(solution)/shard_map/all_to_all | solution.py:143
  58.5 2.1 reshape.395
  60.6 17.1 %all-to-all-done = bf16[128,32,128]{0,2,1:T(8,128)(2,1)S(1)} async-done(((bf16[128,32,128]{0,2,1:T(8,128)(2,1)}), bf16[128,32,128]{0,2,1:T(8,128)(2,1)S(1)}, u32[]{:S(2)}, u32[]{:S(2)}) %all-to-all-start) | async-done | bytes 1048608 | tf_op jit(solution)/shard_map/all_to_all | solution.py:143
  80.0 37.7 %while.24 = (s32[]{:T(128)}, bf16[4,8,64,1,64]{2,4,1,3,0:T(8,128)(2,1)}, f32[4,8,1,64,1,1]{3,1,5,4,2,0:T(8,128)S(1)}, s32[4,8,13]{2,1,0:T(8,128)S(1)}, bf16[32,1...) while((s32[]{:T(128)}, ...), condition=%wide.region_4.5_spmd, body=%wide.region_1.4_spmd.sunk | while | flops 227509056 | bytes 27557372 | solution.py:152
  80.1 2.0 gather_fusion.1
  82.1 2.0 gather_fusion
  84.1 2.3 fusion.78
  87.7 1.7 fusion.79
  89.5 2.0 gather_fusion.1
  91.5 2.0 gather_fusion
  93.5 2.3 fusion.78
  97.1 1.7 fusion.79
  98.9 2.0 gather_fusion.1
  100.9 2.0 gather_fusion
  102.9 2.3 fusion.78
  106.5 1.7 fusion.79
  108.3 2.0 gather_fusion.1
  110.4 2.0 gather_fusion
  112.4 2.3 fusion.78
  116.0 1.7 fusion.79
  117.6 2.0 copy.92
  119.7 2.1 reshape.396
  121.8 9.4 %all-to-all-start.2 = ((bf16[32,2,2048]{2,1,0:T(2,128)(2,1)}), bf16[32,2,2048]{2,1,0:T(2,128)(2,1)}, u32[]{:S(2)}, u32[]{:S(2)}) async-start(bf16[32,2,2048]{2,1,0:T(2,128)(2,1)} %reshape.396), calls=%async_computation.2 | async-start | bytes 524288 | tf_op jit(solution)/shard_map/all_to_all | solution.py:153
  132.8 179.0 %while.25 = (s32[]{:T(128)}, f32[32,128,2,1,64]{1,4,2,0,3:T(8,128)}, bf16[4,8,64,1,64]{4,2,1,0,3:T(8,128)(2,1)}, s32[4,8,13]{2,1,0:T(8,128)S(1)}, bf16[4,8,64,1,...) while((s32[]{:T(128)}, ...), condition=%wide.region_7.8_spmd, body=%wide.region_5.7_spmd.sunk | while | flops 558236480 | bytes 118255368 | solution.py:183
  135.0 2.0 gather_fusion.3
  137.0 2.0 gather_fusion.2
  139.0 2.2 fusion.90
  144.0 2.7 convolution_bitcast_fusion.3
  147.5 2.5 multiply_bitcast_fusion.2
  151.4 3.5 copy.128
  154.9 23.1 %scatter_fusion = f32[32,128,2,64]{1,3,2,0:T(8,128)} fusion(f32[32,128,2,64]{1,3,2,0:T(8,128)} %bitcast.272, s32[104]{0:T(128)S(1)} %reshape.425, f32[104,128,2,64]{1,3,2,0:T(8,128)} %copy.128), kind=kCustom, calls=%fused_computation.4.clone.1 | custom fusion | flops 1703936 | bytes 20447648 | tf_op jit(solution)/shard_map/while/body/eval_jaxpr/scatter-add | solution.py:180
  180.2 2.0 gather_fusion.3
  182.2 2.0 gather_fusion.2
  184.2 2.2 fusion.90
  189.2 2.7 convolution_bitcast_fusion.3
  192.7 2.5 multiply_bitcast_fusion.2
  196.5 3.5 copy.128
  200.1 22.5 %scatter_fusion = f32[32,128,2,64]{1,3,2,0:T(8,128)} fusion(f32[32,128,2,64]{1,3,2,0:T(8,128)} %bitcast.272, s32[104]{0:T(128)S(1)} %reshape.425, f32[104,128,2,64]{1,3,2,0:T(8,128)} %copy.128), kind=kCustom, calls=%fused_computation.4.clone.1 | custom fusion | flops 1703936 | bytes 20447648 | tf_op jit(solution)/shard_map/while/body/eval_jaxpr/scatter-add | solution.py:180
  224.7 2.0 gather_fusion.3
  226.7 2.0 gather_fusion.2
  228.7 2.2 fusion.90
  233.7 2.7 convolution_bitcast_fusion.3
  237.3 2.5 multiply_bitcast_fusion.2
  241.1 3.5 copy.128
  244.6 22.6 %scatter_fusion = f32[32,128,2,64]{1,3,2,0:T(8,128)} fusion(f32[32,128,2,64]{1,3,2,0:T(8,128)} %bitcast.272, s32[104]{0:T(128)S(1)} %reshape.425, f32[104,128,2,64]{1,3,2,0:T(8,128)} %copy.128), kind=kCustom, calls=%fused_computation.4.clone.1 | custom fusion | flops 1703936 | bytes 20447648 | tf_op jit(solution)/shard_map/while/body/eval_jaxpr/scatter-add | solution.py:180
  269.4 2.0 gather_fusion.3
  271.4 2.0 gather_fusion.2
  273.4 2.2 fusion.90
  278.4 2.7 convolution_bitcast_fusion.3
  281.9 2.5 multiply_bitcast_fusion.2
  285.8 3.5 copy.128
  289.3 22.6 %scatter_fusion = f32[32,128,2,64]{1,3,2,0:T(8,128)} fusion(f32[32,128,2,64]{1,3,2,0:T(8,128)} %bitcast.272, s32[104]{0:T(128)S(1)} %reshape.425, f32[104,128,2,64]{1,3,2,0:T(8,128)} %copy.128), kind=kCustom, calls=%fused_computation.4.clone.1 | custom fusion | flops 1703936 | bytes 20447648 | tf_op jit(solution)/shard_map/while/body/eval_jaxpr/scatter-add | solution.py:180
  313.3 17.3 %all_to_all.90 = bf16[32,2,2048]{2,1,0:T(2,128)(2,1)S(1)} all-to-all(bf16[32,2,2048]{2,1,0:T(2,128)(2,1)S(1)} %reshape.400), channel_id=1, replica_groups=mesh['dp'=8,'seq'=32] {'seq'}, dimensions={0} | all-to-all | bytes 524288 | tf_op jit(solution)/shard_map/all_to_all | solution.py:195
  330.6 6.2 all-to-all-start.5
  338.9 2.7 fusion.42
  344.6 279.6 %all-reduce.2.cloned.1.call-done = f32[1024,1024]{1,0:T(8,128)} async-done(((f32[1024,1024]{1,0:T(8,128)}), f32[1024,1024]{1,0:T(8,128)}) %all-reduce.2.cloned.1.call-update) | async-done | bytes 4194320 | tf_op jit(solution)/shard_map/psum | solution.py:220
  625.8 1.8 reduce_sum.18
  (183 shorter events, 57.1 us)
Async XLA Ops:
  7.2 1.6 copy-start
  12.2 19.3 %all-to-all-start.3 = ((bf16[32,2,2048]{2,1,0:T(2,128)(2,1)}), bf16[32,2,2048]{2,1,0:T(2,128)(2,1)S(1)}, u32[]{:S(2)}, u32[]{:S(2)}) async-start(bf16[32,2,2048]{2,1,0:T(2,128)(2,1)} %reshape.398), calls=%async_computation.3 | async-start | bytes 524288 | tf_op jit(solution)/shard_map/all_to_all | solution.py:164
  24.8 31.1 %copy-start.11 = (s32[1,32,4]{1,2,0:T(4,128)S(1)}, s32[1,32,4]{1,2,0:T(4,128)}, u32[]{:S(2)}) copy-start(s32[1,32,4]{1,2,0:T(4,128)} %param.17) | copy-start | bytes 1540
  24.8 31.4 %copy-start.10 = (s32[1,32,8]{1,2,0:T(8,128)S(1)}, s32[1,32,8]{1,2,0:T(8,128)}, u32[]{:S(2)}) copy-start(s32[1,32,8]{1,2,0:T(8,128)} %param.18) | copy-start | bytes 3076
  25.9 30.5 %copy-start.12 = (s32[1,32]{1,0:T(1,128)S(1)}, s32[1,32]{1,0:T(1,128)}, u32[]{:S(2)}) copy-start(s32[1,32]{1,0:T(1,128)} %param.19) | copy-start | bytes 388
  31.6 16.0 %all-to-all-start.1 = ((bf16[32,2,2048]{2,1,0:T(2,128)(2,1)}), bf16[32,2,2048]{2,1,0:T(2,128)(2,1)S(1)}, u32[]{:S(2)}, u32[]{:S(2)}) async-start(bf16[32,2,2048]{2,1,0:T(2,128)(2,1)} %reshape.394), calls=%async_computation.1 | async-start | bytes 524288 | tf_op jit(solution)/shard_map/all_to_all | solution.py:129
  47.5 1.2 copy-start.9
  48.8 28.9 %all-to-all-start = ((bf16[128,32,128]{0,2,1:T(8,128)(2,1)}), bf16[128,32,128]{0,2,1:T(8,128)(2,1)S(1)}, u32[]{:S(2)}, u32[]{:S(2)}) async-start(bf16[128,32,128]{0,2,1:T(8,128)(2,1)} %bitcast.288), calls=%async_computation | async-start | bytes 2097152 | tf_op jit(solution)/shard_map/all_to_all | solution.py:143
  77.7 1.0 copy-start.7
  84.1 3.6 copy-start.3
  93.5 3.6 copy-start.3
  102.9 3.6 copy-start.3
  112.4 3.6 copy-start.3
  121.8 191.5 %all-to-all-start.2 = ((bf16[32,2,2048]{2,1,0:T(2,128)(2,1)}), bf16[32,2,2048]{2,1,0:T(2,128)(2,1)}, u32[]{:S(2)}, u32[]{:S(2)}) async-start(bf16[32,2,2048]{2,1,0:T(2,128)(2,1)} %reshape.396), calls=%async_computation.2 | async-start | bytes 524288 | tf_op jit(solution)/shard_map/all_to_all | solution.py:153
  139.0 2.3 copy-start.4
  139.0 2.3 copy-start.6
  141.3 1.5 copy-start.1
  142.7 1.3 copy-start.5
  146.9 3.2 copy-start.2
  184.2 2.3 copy-start.4
  184.2 2.3 copy-start.6
  186.4 1.5 copy-start.1
  187.9 1.3 copy-start.5
  192.0 3.2 copy-start.2
  228.7 2.3 copy-start.4
  228.7 2.3 copy-start.6
  231.0 1.5 copy-start.1
  232.5 1.3 copy-start.5
  236.6 3.2 copy-start.2
  273.4 2.3 copy-start.4
  273.4 2.3 copy-start.6
  275.7 1.5 copy-start.1
  277.1 1.3 copy-start.5
  281.3 3.2 copy-start.2
  330.6 8.3 %copy-start.8 = (bf16[1,128,1024]{2,1,0:T(8,128)(2,1)S(1)}, bf16[1,128,1024]{2,1,0:T(8,128)(2,1)}, u32[]{:S(2)}) copy-start(bf16[1,128,1024]{2,1,0:T(8,128)(2,1)} %param.15) | copy-start | bytes 786436
  330.6 295.2 %all-to-all-start.5 = ((f32[32,128,1,128]{1,3,2,0:T(8,128)}), f32[32,128,1,128]{1,3,2,0:T(8,128)}, u32[]{:S(2)}, u32[]{:S(2)}) async-start(f32[32,128,1,128]{1,3,2,0:T(8,128)} %bitcast.274), calls=%async_computation.5 | async-start | bytes 4194304 | tf_op jit(solution)/shard_map/all_to_all | solution.py:203
  336.8 287.4 %all-reduce.2.cloned.1.call-start = ((), (), s32[]{:S(2)}) async-start(), calls=%async_computation.6 | async-start | bytes 8388608 | tf_op jit(solution)/shard_map/psum | solution.py:220
Sparse Core Ops, SparseCore 0:
  343.1 281.0 all-reduce.1
where the time goes:
time: 640 us; the launch traced here: 636 us
  waiting for transfers between devices  307 us (48%)
  other arithmetic  110 us (17%)
  local copies, waits for them, and re-layouts  86.3 us (13%)
  matrix products  59.3 us (9%)
  starting transfers between devices  41.4 us (6%)
  blocking collectives  17.3 us (3%)
  between operations  14.3 us (2%)
    psum x1, waiting for transfers between devices, local(): summed_whole = lax.psum(whole, ('dp', 'seq'))  280 us
    scatter-add x4, other arithmetic, backward_step(): return (running.at[table_group].add(terms), query_part)  90.7 us
    dot_general x8, matrix products, scores_for(): jnp.einsum('bqpd,bskpd->bpqsk', query_group, selected_key_rows, preferred...  18.2 us
    unnamed x27, local copies, waits for them, and re-layouts  18.1 us
    all_to_all x1, blocking collectives, local(): lax.all_to_all(query_parts.reshape(seq_size, local_rows, 1, group_width),...  17.3 us
    all_to_all x1, waiting for transfers between devices, local(): lax.all_to_all(key_value, 'seq', split_axis=1, concat_axis=0, tiled=True)  17.1 us
    another operation x4, local copies, waits for them, and re-layouts, backward_group(): jnp.stack([key_products, value_products], axis=3)  14.1 us
  transfers between devices with their start and end apart: 6, of which 4 were waited for; matrix products, arithmetic and copies ran while one was open for 31% of the time, Pallas kernels for 0%

commit v1 on v0

v1 whole, which is shorter than its diff:
```python
import functools

import jax
import jax.numpy as jnp
from jax import lax
from jax.experimental import pallas as pl
from jax.experimental.pallas import tpu as pltpu
from jax.sharding import PartitionSpec as P

HEADS = 16
HDIM = 64
BLK = 128
NB = 32
HALF = 16
GROUP = 2
SLOTS = 16
MESH = pl.DeviceIdType.MESH
VMEM = pltpu.VMEM
BF = jnp.bfloat16
F32 = jnp.float32


def place():
    dp = lax.axis_index("dp")
    s = lax.axis_index("seq")
    return dp // 2, dp % 2, s


def partner(x, c, s, j):
    return (x * 2 + s % 2, 2 * j + c)


def greet(x, c, s):
    barrier = pltpu.get_barrier_semaphore()
    alone = c == s % 2

    @pl.loop(0, HALF)
    def _(j):
        @pl.when(jnp.logical_not(jnp.logical_and(alone, j == s // 2)))
        def _():
            pl.semaphore_signal(barrier, inc=1, device_id=partner(x, c, s, j), device_id_type=MESH)

    pl.semaphore_signal(barrier, inc=1, device_id=(x * 2 + 1 - c, s), device_id_type=MESH)
    pl.semaphore_wait(barrier, jnp.where(alone, HALF, HALF + 1))


def scatter_kernel(
    q_ref, k_ref, v_ref, cot_ref, w_ref, tab_ref,
    kv_ref, qd_ref, tabo_ref,
    send_kv, send_qd, tab_sib,
    kv_ss, kv_rs, qd_ss, qd_rs, re_ss, re_rs, tb_ss, tb_rs,
):
    x, c, s = place()
    alone = c == s % 2
    mine = s // 2
    sibling = (x * 2 + 1 - c, s)
    greet(x, c, s)

    def is_self(j):
        return jnp.logical_and(alone, j == mine)

    tab_copy = pltpu.make_async_remote_copy(
        src_ref=tab_ref, dst_ref=tab_sib, send_sem=tb_ss, recv_sem=tb_rs,
        device_id=sibling, device_id_type=MESH)
    tab_copy.start()

    def kv_out(j):
        return pltpu.make_async_remote_copy(
            src_ref=send_kv.at[j], dst_ref=kv_ref.at[s], send_sem=kv_ss.at[j], recv_sem=kv_rs.at[mine],
            device_id=partner(x, c, s, j), device_id_type=MESH)

    def qd_out(j):
        return pltpu.make_async_remote_copy(
            src_ref=send_qd.at[j], dst_ref=qd_ref.at[mine], send_sem=qd_ss.at[j], recv_sem=qd_rs.at[mine],
            device_id=partner(x, c, s, j), device_id_type=MESH)

    def kv_in(j):
        return pltpu.make_async_remote_copy(
            src_ref=send_kv.at[j], dst_ref=kv_ref.at[2 * j + c], send_sem=kv_ss.at[j], recv_sem=kv_rs.at[j],
            device_id=partner(x, c, s, j), device_id_type=MESH)

    def qd_in(j):
        return pltpu.make_async_remote_copy(
            src_ref=send_qd.at[j], dst_ref=qd_ref.at[j], send_sem=qd_ss.at[j], recv_sem=qd_rs.at[j],
            device_id=partner(x, c, s, j), device_id_type=MESH)

    def relay(j, odd):
        return pltpu.make_async_remote_copy(
            src_ref=kv_ref.at[2 * j + odd], dst_ref=kv_ref.at[2 * j + odd], send_sem=re_ss.at[j], recv_sem=re_rs.at[j],
            device_id=sibling, device_id_type=MESH)

    @pl.loop(0, HEADS // 2)
    def _(t):
        pair = (t + s // 4) % (HEADS // 2)
        cols = pl.ds(pl.multiple_of(pair * 128, 128), 128)
        k = k_ref[:, cols]
        v = v_ref[:, cols]
        for e in range(2):
            j = pair * 2 + e
            send_kv[j] = jnp.concatenate([k[:, e * 64:e * 64 + 64], v[:, e * 64:e * 64 + 64]], axis=1)

            @pl.when(jnp.logical_not(is_self(j)))
            def _():
                kv_out(j).start()

            @pl.when(is_self(j))
            def _():
                kv_ref[s] = send_kv[j]

    @pl.loop(0, HEADS // 2)
    def _(t):
        pair = (t + s // 4) % (HEADS // 2)
        cols = pl.ds(pl.multiple_of(pair * 128, 128), 128)
        q = q_ref[:, cols] * jnp.asarray(0.125, BF)
        d = lax.dot_general(cot_ref[...], w_ref[cols, :], (((1,), (1,)), ((), ())),
                            preferred_element_type=F32).astype(BF)
        for e in range(2):
            j = pair * 2 + e
            send_qd[j] = jnp.concatenate([q[:, e * 64:e * 64 + 64], d[:, e * 64:e * 64 + 64]], axis=1)

            @pl.when(jnp.logical_not(is_self(j)))
            def _():
                qd_out(j).start()

            @pl.when(is_self(j))
            def _():
                qd_ref[mine] = send_qd[j]

    @pl.loop(0, HALF)
    def _(t):
        j = (t + mine) % HALF

        @pl.when(jnp.logical_not(is_self(j)))
        def _():
            kv_in(j).wait_recv()

        relay(j, c).start()

    tab_copy.wait()
    own = jnp.broadcast_to(alone.astype(jnp.int32), tab_ref.shape)
    tabo_ref[...] = tab_ref[...] * own + tab_sib[...] * (1 - own)

    @pl.loop(0, HALF)
    def _(t):
        j = (t + mine) % HALF
        relay(j, 1 - c).wait_recv()

        @pl.when(jnp.logical_not(is_self(j)))
        def _():
            qd_in(j).wait_recv()

    @pl.loop(0, HALF)
    def _(j):
        relay(j, c).wait_send()

        @pl.when(jnp.logical_not(is_self(j)))
        def _():
            kv_out(j).wait_send()
            qd_out(j).wait_send()


def core_kernel(tab_ref, kv_ref, qd_ref, par_ref, out_ref, dkv_ref, kvt, acc, sbuf, pbuf, qd2, qd2t, slots):
    c = par_ref[0]

    @pl.loop(0, NB)
    def _(b):
        kvt[b] = kv_ref[b].T
        acc[b] = jnp.zeros((BLK, BLK), F32)

    qd2[...] = jnp.zeros((2 * BLK, BLK), BF)
    qd2t[...] = jnp.zeros((BLK, 2 * BLK), BF)
    rows = GROUP * BLK

    @pl.loop(0, HALF)
    def _(i):
        b = 2 * i + c
        owner = tab_ref[b, 12]
        for e in range(SLOTS):
            slots[e] = b
        n = jnp.int32(1)
        for e in range(12):
            other = tab_ref[b, e]
            good = other >= 0
            if e >= 4:
                good = jnp.logical_and(good, tab_ref[jnp.maximum(other, 0), 12] != owner)
            slots[n] = jnp.where(good, other, b)
            n = n + good.astype(jnp.int32)
        steps = (n + GROUP - 1) // GROUP

        qd = qd_ref[i]
        qdt = qd.T
        qd2[0:BLK, 0:HDIM] = qd[:, 0:HDIM]
        qd2[BLK:, HDIM:] = qd[:, HDIM:]
        qd2t[0:HDIM, 0:BLK] = qdt[0:HDIM, :]
        qd2t[HDIM:, BLK:] = qdt[HDIM:, :]

        def scores(g, m):
            keys = jnp.concatenate([kv_ref[slots[g * GROUP + u]] for u in range(GROUP)], axis=0)
            both = jnp.dot(keys, qd2t[...], preferred_element_type=F32)
            for u in range(GROUP):
                bias = jnp.where(g * GROUP + u < n, 0.0, -jnp.inf).astype(F32)
                part = both[u * BLK:(u + 1) * BLK, 0:BLK] + bias
                sbuf[g * GROUP + u] = part
                pbuf[g * GROUP + u] = both[u * BLK:(u + 1) * BLK, BLK:]
                m = jnp.maximum(m, jnp.max(part.reshape(BLK // 8, 8, BLK), axis=0))
            return m

        m = lax.fori_loop(0, steps, scores, jnp.full((8, BLK), -jnp.inf, F32))
        m = jnp.broadcast_to(jnp.max(m, axis=0, keepdims=True), (8, BLK))

        def weigh(g, carry):
            total, dot = carry
            for u in range(GROUP):
                part = jnp.exp(sbuf[g * GROUP + u].reshape(BLK // 8, 8, BLK) - m[None])
                sbuf[g * GROUP + u] = part.reshape(BLK, BLK)
                total = total + jnp.sum(part, axis=0)
                dot = dot + jnp.sum(part * pbuf[g * GROUP + u].reshape(BLK // 8, 8, BLK), axis=0)
            return total, dot

        zero = jnp.zeros((8, BLK), F32)
        total, dot = lax.fori_loop(0, steps, weigh, (zero, zero))
        inv = 1.0 / jnp.sum(total, axis=0, keepdims=True)
        delta = jnp.broadcast_to(jnp.sum(dot, axis=0, keepdims=True) * inv, (8, BLK))
        inv = jnp.broadcast_to(inv, (8, BLK))

        def grads(g, carry):
            dq, at = carry
            parts = []
            for u in range(GROUP):
                prob = sbuf[g * GROUP + u].reshape(BLK // 8, 8, BLK) * inv[None]
                ds = prob * (pbuf[g * GROUP + u].reshape(BLK // 8, 8, BLK) - delta[None])
                parts.append(jnp.concatenate(
                    [ds.reshape(BLK, BLK).astype(BF), prob.reshape(BLK, BLK).astype(BF)], axis=1))
            both = jnp.concatenate(parts, axis=0)
            dkv = jnp.dot(both, qd2[...], preferred_element_type=F32)
            for u in range(GROUP):
                other = slots[g * GROUP + u]
                acc[other] = acc[other] + dkv[u * BLK:(u + 1) * BLK]
            keys = jnp.concatenate([kvt[slots[g * GROUP + u]] for u in range(GROUP)], axis=1)
            mixed = jnp.dot(keys, both, preferred_element_type=F32)
            return dq + mixed[0:HDIM, 0:BLK], at + mixed[HDIM:, BLK:]

        zero = jnp.zeros((HDIM, BLK), F32)
        dq, at = lax.fori_loop(0, steps, grads, (zero, zero))
        out_ref[i] = jnp.concatenate([dq * 0.125, at], axis=0).T.astype(BF)

    @pl.loop(0, HALF)
    def _(i):
        for e in range(2):
            dkv_ref[e, i] = acc[2 * i + e].astype(BF)


def gather_kernel(
    od_ref, dkv_ref, w_ref,
    o_ref, dq_ref, dk_ref, dv_ref, at_ref,
    ret_a, ret_b, sib, send_b,
    a_ss, a_rs, b_ss, b_rs, s_ss, s_rs,
):
    x, c, s = place()
    alone = c == s % 2
    mine = s // 2
    sibling = (x * 2 + 1 - c, s)
    greet(x, c, s)

    def is_self(j):
        return jnp.logical_and(alone, j == mine)

    def a_copy(j, slot):
        return pltpu.make_async_remote_copy(
            src_ref=od_ref.at[j], dst_ref=ret_a.at[slot], send_sem=a_ss.at[j], recv_sem=a_rs.at[slot],
            device_id=partner(x, c, s, j), device_id_type=MESH)

    def b_copy(j, slot):
        return pltpu.make_async_remote_copy(
            src_ref=send_b.at[j], dst_ref=ret_b.at[slot], send_sem=b_ss.at[j], recv_sem=b_rs.at[slot],
            device_id=partner(x, c, s, j), device_id_type=MESH)

    def s_copy(r):
        return pltpu.make_async_remote_copy(
            src_ref=dkv_ref.at[1 - c, pl.ds(r * 4, 4)], dst_ref=sib.at[pl.ds(r * 4, 4)],
            send_sem=s_ss.at[r], recv_sem=s_rs.at[r],
            device_id=sibling, device_id_type=MESH)

    @pl.loop(0, 4)
    def _(t):
        s_copy((t + s // 8) % 4).start()

    @pl.loop(0, HALF)
    def _(t):
        j = (t + mine) % HALF

        @pl.when(jnp.logical_not(is_self(j)))
        def _():
            a_copy(j, mine).start()

        @pl.when(is_self(j))
        def _():
            ret_a[mine] = od_ref[j]

    @pl.loop(0, 4)
    def _(t):
        r = (t + s // 8) % 4
        s_copy(r).wait_recv()

        @pl.loop(0, 4)
        def _(u):
            j = r * 4 + u
            send_b[j] = (dkv_ref[c, j].astype(F32) + sib[j].astype(F32)).astype(BF)

            @pl.when(jnp.logical_not(is_self(j)))
            def _():
                b_copy(j, mine).start()

            @pl.when(is_self(j))
            def _():
                ret_b[mine] = send_b[j]

    @pl.loop(0, HEADS // 2)
    def _(pair):
        cols = pl.ds(pl.multiple_of(pair * 128, 128), 128)
        for e in range(2):
            @pl.when(jnp.logical_not(is_self(pair * 2 + e)))
            def _():
                a_copy(pair * 2 + e, pair * 2 + e).wait_recv()

        a0 = ret_a[pair * 2]
        a1 = ret_a[pair * 2 + 1]
        dq_ref[:, cols] = jnp.concatenate([a0[:, 0:64], a1[:, 0:64]], axis=1)
        at_ref[:, cols] = jnp.concatenate([a0[:, 64:], a1[:, 64:]], axis=1)

    @pl.loop(0, 4)
    def _(t):
        cols = pl.ds(pl.multiple_of(t * 256, 256), 256)
        o_ref[:, cols] = jnp.dot(at_ref[...], w_ref[:, cols], preferred_element_type=F32).astype(BF)

    @pl.loop(0, HEADS // 2)
    def _(pair):
        cols = pl.ds(pl.multiple_of(pair * 128, 128), 128)
        for e in range(2):
            @pl.when(jnp.logical_not(is_self(pair * 2 + e)))
            def _():
                b_copy(pair * 2 + e, pair * 2 + e).wait_recv()

        a0 = ret_b[pair * 2]
        a1 = ret_b[pair * 2 + 1]
        dk_ref[:, cols] = jnp.concatenate([a0[:, 0:64], a1[:, 0:64]], axis=1)
        dv_ref[:, cols] = jnp.concatenate([a0[:, 64:], a1[:, 64:]], axis=1)

    @pl.loop(0, HALF)
    def _(j):
        @pl.when(jnp.logical_not(is_self(j)))
        def _():
            a_copy(j, mine).wait_send()
            b_copy(j, mine).wait_send()

    @pl.loop(0, 4)
    def _(r):
        s_copy(r).wait_send()


def spec(n):
    return [pl.BlockSpec(memory_space=VMEM)] * n


def attend(tab, kv, qd, parity):
    tile = lambda n, t: jax.ShapeDtypeStruct((n, BLK, BLK), t)
    return pl.pallas_call(
        core_kernel,
        out_shape=(tile(HALF, BF), jax.ShapeDtypeStruct((2, HALF, BLK, BLK), BF)),
        in_specs=[pl.BlockSpec(memory_space=pltpu.SMEM)] + spec(2) + [pl.BlockSpec(memory_space=pltpu.SMEM)],
        out_specs=tuple(spec(2)),
        scratch_shapes=[
            VMEM((NB, BLK, BLK), BF), VMEM((NB, BLK, BLK), F32),
            VMEM((SLOTS, BLK, BLK), F32), VMEM((SLOTS, BLK, BLK), F32),
            VMEM((2 * BLK, BLK), BF), VMEM((BLK, 2 * BLK), BF),
            pltpu.SMEM((SLOTS,), jnp.int32),
        ],
        compiler_params=pltpu.CompilerParams(vmem_limit_bytes=32 * 2**20),
        name="attend",
    )(tab, kv, qd, parity)


def local(node_queries, node_keys, node_values, cotangent, w_out, neighbours, contacts, ownership):
    tile = lambda n, t: jax.ShapeDtypeStruct((n, BLK, BLK), t)
    flat = jax.ShapeDtypeStruct((BLK, HEADS * HDIM), BF)
    dma = pltpu.SemaphoreType.DMA
    table = jnp.concatenate([neighbours[0], contacts[0], ownership[0][:, None]], axis=1)
    table = jnp.pad(table, ((0, 0), (0, 128 - 13)))
    kv, qd, tab = pl.pallas_call(
        scatter_kernel,
        out_shape=(tile(NB, BF), tile(HALF, BF), jax.ShapeDtypeStruct((NB, 128), jnp.int32)),
        in_specs=spec(6),
        out_specs=tuple(spec(3)),
        scratch_shapes=[
            VMEM((HALF, BLK, BLK), BF), VMEM((HALF, BLK, BLK), BF), VMEM((NB, 128), jnp.int32),
            dma((HALF,)), dma((HALF,)), dma((HALF,)), dma((HALF,)), dma((HALF,)), dma((HALF,)), dma, dma,
        ],
        compiler_params=pltpu.CompilerParams(
            collective_id=0, has_side_effects=True, vmem_limit_bytes=32 * 2**20),
        name="scatter_heads",
    )(node_queries[0], node_keys[0], node_values[0], cotangent[0], w_out, table)

    parity = (lax.axis_index("dp") % 2).astype(jnp.int32).reshape(1)
    od, dkv = attend(tab, kv, qd, parity)

    output, dq, dk, dv, att = pl.pallas_call(
        gather_kernel,
        out_shape=(flat,) * 5,
        in_specs=spec(3),
        out_specs=tuple(spec(5)),
        scratch_shapes=[
            VMEM((HALF, BLK, BLK), BF), VMEM((HALF, BLK, BLK), BF), VMEM((HALF, BLK, BLK), BF), VMEM((HALF, BLK, BLK), BF),
            dma((HALF,)), dma((HALF,)), dma((HALF,)), dma((HALF,)), dma((4,)), dma((4,)),
        ],
        compiler_params=pltpu.CompilerParams(
            collective_id=1, has_side_effects=True, vmem_limit_bytes=32 * 2**20),
        name="gather_nodes",
    )(od, dkv, w_out)

    scenes = lax.axis_size("dp")
    cot_all = lax.all_gather(cotangent[0], "dp", axis=0, tiled=True)
    share = att.reshape(BLK, NB, scenes, NB // scenes)
    share = lax.all_to_all(share, "dp", split_axis=2, concat_axis=0, tiled=True)
    share = share.reshape(scenes * BLK, NB * (NB // scenes))
    part = lax.dot_general(share, cot_all, (((0,), (0,)), ((), ())), preferred_element_type=F32)
    part = lax.psum_scatter(part.reshape(NB, (NB // scenes) * 1024), "seq", scatter_dimension=0, tiled=True)
    weight_grad = lax.all_gather(part.reshape(NB // scenes, 1024), "dp", axis=0, tiled=True)
    weight_grad = weight_grad * (scenes * NB * BLK) ** (-0.5)
    return (output[None], dq[None], dk[None], dv[None], weight_grad)


def solution(mesh):
    placed = (
        P("dp", "seq", None), P("dp", "seq", None), P("dp", "seq", None), P("dp", "seq", None),
        P(), P("dp", None, None), P("dp", None, None), P("dp", None),
    )
    return jax.shard_map(
        local,
        mesh=mesh,
        in_specs=placed,
        out_specs=(
            P("dp", "seq", None), P("dp", "seq", None), P("dp", "seq", None), P("dp", "seq", None),
            P("seq", None),
        ),
        check_vma=False,
    )
```

time: 640 us -> 302 us (0.47)
  waiting for transfers between devices: 307 us -> 142 us
  other arithmetic: 110 us -> 0.11 us
  Pallas kernels: 0 us -> 95.6 us
  local copies, waits for them, and re-layouts: 86.3 us -> 15 us
  matrix products: 59.3 us -> 2.04 us
  starting transfers between devices: 41.4 us -> 0.08 us
  blocking collectives: 17.3 us -> 29.9 us
    psum x1 -> x0, waiting for transfers between devices: 280 us -> none  [local(): summed_whole = lax.psum(whole, ('dp', 'seq'))]
    unnamed x1 -> x3, waiting for transfers between devices: 0.02 us -> 142 us
    pallas_call x0 -> x3, Pallas kernels: none -> 95.6 us  [the longest x1 33.6 us: local(): pl.pallas_call(scatter_kernel, out_shape=(tile(NB, BF), tile(HALF, BF), j...]
    scatter-add x4 -> x0, other arithmetic: 90.7 us -> none  [backward_step(): return (running.at[table_group].add(terms), query_part)]
    dot_general x31 -> x1, matrix products: 59.3 us -> 2.04 us  [local(): lax.dot_general(share, cot_all, (((0,), (0,)), ((), ())), preferred_eleme...]
    all_to_all x5 -> x0, starting transfers between devices: 41.3 us -> none  [the longest x1 11 us: local(): lax.all_to_all(to_heads(attention_grad), 'seq', split_axis=1, concat_axis...]
    gather x16 -> x0, local copies, waits for them, and re-layouts: 32.1 us -> none  [the longest x4 8.16 us: forward_group(): selected_key_rows = key_blocks[table_group]]
    all_to_all x5 -> x0, waiting for transfers between devices: 27.1 us -> none  [the longest x1 17.1 us: local(): lax.all_to_all(key_value, 'seq', split_axis=1, concat_axis=0, tiled=True)]
  transfers between devices with their start and end apart: 6 -> 2, of which waited for: 4 -> 1; matrix products, arithmetic and copies ran while one was open for 31% -> 1% of each run, Pallas kernels for 0% -> 32%
where the time goes in v1:
time: 302 us; the launch traced here: 299 us
  waiting for transfers between devices  142 us (47%)
  Pallas kernels  95.6 us (32%)
  blocking collectives  29.9 us (10%)
  local copies, waits for them, and re-layouts  15 us (5%)
  between operations  14.2 us (5%)
    unnamed x3, waiting for transfers between devices  142 us
    pallas_call x1, Pallas kernels, local(): pl.pallas_call(scatter_kernel, out_shape=(tile(NB, BF), tile(HALF, BF), j...  33.6 us
    pallas_call x1, Pallas kernels, attend(): pl.pallas_call(core_kernel, out_shape=(tile(HALF, BF), jax.ShapeDtypeStru...  32 us
    pallas_call x1, Pallas kernels, local(): pl.pallas_call(gather_kernel, out_shape=(flat,) * 5, in_specs=spec(3), ou...  30 us
    all_gather x1, blocking collectives, local(): lax.all_gather(part.reshape(NB // scenes, 1024), 'dp', axis=0, tiled=True)  17.9 us
    all_to_all x1, blocking collectives, local(): share = lax.all_to_all(share, 'dp', split_axis=2, concat_axis=0, tiled=True)  12 us
    unnamed x22, local copies, waits for them, and re-layouts  11.2 us
  transfers between devices with their start and end apart: 2, of which 1 were waited for; matrix products, arithmetic and copies ran while one was open for 1% of the time, Pallas kernels for 32%

profile of v1, /device:TPU:17, one launch (start us, length us, event | category | flops | bytes accessed | tf_op | source)
XLA Modules:
  0.0 298.7 jit_solution(5790633517834022091)
XLA Ops:
  7.2 0.0 all-gather.4.cloned.1.call-start
  7.2 0.7 all-gather.4.cloned.1.call-update
  7.9 0.0 all-reduce.4.cloned.1.call-start
  8.0 0.7 copy.23
  8.7 0.8 copy.21
  9.5 0.8 copy.22
  10.2 0.1 pad_add_fusion
  10.3 0.0 copy-start
  10.3 1.6 copy-done
  11.9 0.0 copy-start.2
  11.9 0.9 copy-done.2
  12.9 0.0 copy-start.3
  12.9 0.9 copy-done.3
  13.8 0.0 copy-start.4
  13.8 0.9 copy-done.4
  14.8 0.0 copy-start.5
  14.8 0.9 copy-done.5
  15.7 0.0 copy-start.1
  15.7 33.6 %scatter_heads.1 = (bf16[32,128,128]{2,1,0:T(8,128)(2,1)S(1)}, bf16[16,128,128]{2,1,0:T(8,128)(2,1)S(1)}, s32[32,128]{1,0:T(8,128)S(1)}) custom-call(bf16[128,1024]{1,0:T(8,128)(2,1)S(1)} %bitcast.28, bf16[128,1024]{1,0:T(8,128)(2,1)S(1)} %bitcast.29, bf16[128,1024]{1,0:T(8,128)(2,1)S(1)} %bitcast.30, bf16[128,1024]{1,0:T(8,128)(2,1)S(1)} %bitcast.27, ...), custom_call_target="tpu_custom_call" | custom-call | tf_op jit(solution)/shard_map/scatter_heads/pallas_call | solution.py:389
  49.3 32.0 %attend.1 = (bf16[16,128,128]{2,1,0:T(8,128)(2,1)S(1)}, bf16[2,16,128,128]{3,2,1,0:T(8,128)(2,1)S(1)}) custom-call(s32[32,128]{1,0:T(8,128)S(1)} %get-tuple-element.15.tab_ref, bf16[32,128,128]{2,1,0:T(8,128)(2,1)S(1)} %get-tuple-element.16.kv_ref, bf16[16,128,128]{2,1,0:T(8,128)(2,1)S(1)} %get-tuple-element.17.qd_ref, s32[1]{0:T(128)} %bitcast.7.par_ref), custom_call_target="tpu_custom_call" | custom-call | tf_op jit(solution)/shard_map/attend/pallas_call | solution.py:367
  81.3 0.0 copy-done.1
  81.3 30.0 %gather_nodes.1 = (bf16[128,1024]{1,0:T(8,128)(2,1)S(1)}, bf16[128,1024]{1,0:T(8,128)(2,1)S(1)}, bf16[128,1024]{1,0:T(8,128)(2,1)S(1)}, bf16[128,1024]{1,0:T(8,128)(2,1)S(1)}, bf16[128,1024]{1,0:T(8,128)(2,1)S(1)}) custom-call(bf16[16,128,128]{2,1,0:T(8,128)(2,1)S(1)} %get-tuple-element.18.od_ref, bf16[2,16,128,128]{3,2,1,0:T(8,128)(2,1)S(1)} %get-tuple-element.19.dkv_ref, ...), custom_call_target="tpu_custom_call" | custom-call | tf_op jit(solution)/shard_map/gather_nodes/pallas_call | solution.py:406
  111.3 0.2 copy.24
  111.5 0.1 copy.25
  111.6 12.0 %all_to_all.15 = bf16[128,32,8,4]{0,3,1,2:T(4,128)(2,1)S(1)} all-to-all(bf16[128,32,8,4]{0,3,1,2:T(4,128)(2,1)S(1)} %copy.25), channel_id=1, replica_groups=mesh['dp'=8,'seq'=32] {'dp'}, dimensions={2} | all-to-all | bytes 524288 | tf_op jit(solution)/shard_map/all_to_all | solution.py:423
  123.6 0.3 copy.26
  123.9 0.0 all-gather.4.cloned.1.call-done
  123.9 0.0 copy-start.6
  123.9 2.0 fusion
  126.0 1.0 reshape.29
  127.0 0.0 all-reduce.4.cloned.1.call-update
  127.0 0.0 copy-done.6
  127.0 0.6 dynamic-slice
  127.6 141.2 %all-reduce.4.cloned.1.call-done = f32[32,4096]{1,0:T(8,128)} async-done(((f32[32,4096]{1,0:T(8,128)}), f32[32,4096]{1,0:T(8,128)}) %all-reduce.4.cloned.1.call-update) | async-done | bytes 524304
  268.8 1.6 dynamic-slice_reduce_fusion
  270.4 17.9 %all-gather.1 = f32[8,4,1024]{2,1,0:T(4,128)S(1)} all-gather(f32[1,4,1024]{2,1,0:T(4,128)S(1)} %reshape.32), channel_id=1, replica_groups=mesh['dp'=8,'seq'=32] {'dp'}, dimensions={0}, use_global_device_ids=true | all-gather | bytes 147456 | tf_op jit(solution)/shard_map/all_gather | solution.py:427
  288.4 0.7 reshape.35
  289.1 0.7 copy.37
  289.8 0.7 copy.38
  290.5 0.7 copy.39
  291.2 0.7 copy.40
  (3 shorter events, 0.1 us)
Async XLA Ops:
  7.2 116.8 %all-gather.4.cloned.1.call-start = ((), (), s32[]{:S(2)}) async-start(), calls=%async_computation.1 | async-start | bytes 2359296 | tf_op jit(solution)/shard_map/all_gather | solution.py:421
  7.9 260.9 %all-reduce.4.cloned.1.call-start = ((), (), s32[]{:S(2)}) async-start(), calls=%async_computation.2 | async-start | bytes 1048576
  10.3 1.6 copy-start
  11.9 0.9 copy-start.2
  12.9 0.9 copy-start.3
  13.8 0.9 copy-start.4
  14.8 0.9 copy-start.5
  15.7 65.6 %copy-start.1 = (bf16[1024,1024]{1,0:T(8,128)(2,1)S(1)}, bf16[1024,1024]{1,0:T(8,128)(2,1)}, u32[]{:S(2)}) copy-start(bf16[1024,1024]{1,0:T(8,128)(2,1)} %w_ref.3) | copy-start | bytes 6291460
  123.9 3.1 %copy-start.6 = (u32[256]{0:T(256)S(1)}, u32[256]{0:T(256)}, u32[]{:S(2)}) copy-start(u32[256]{0:T(256)} %constant.33) | copy-start | bytes 3076
Sparse Core Ops, SparseCore 0:
  9.9 30.8 all-gather.3
  127.2 141.6 all-reduce.3

commit v2 on v1

--- a/solution.py
+++ b/solution.py
@@ -11,6 +11,7 @@
 HDIM = 64
 BLK = 128
 NB = 32
+SCENES = 8
 HALF = 16
 GROUP = 2
 SLOTS = 16
@@ -250,17 +251,55 @@
             dkv_ref[e, i] = acc[2 * i + e].astype(BF)
 
 
+def greet_all(x, c, s):
+    barrier = pltpu.get_barrier_semaphore()
+    alone = c == s % 2
+    dp = x * 2 + c
+
+    def hello(device):
+        pl.semaphore_signal(barrier, inc=1, device_id=device, device_id_type=MESH)
+
+    @pl.loop(0, HALF)
+    def _(j):
+        @pl.when(jnp.logical_not(jnp.logical_and(alone, j == s // 2)))
+        def _():
+            hello(partner(x, c, s, j))
+
+    @pl.loop(1, SCENES)
+    def _(t):
+        hello(((dp + t) % SCENES, s))
+
+    @pl.loop(1, NB)
+    def _(t):
+        hello((dp, (s + t) % NB))
+
+    owner = s // 4
+
+    @pl.loop(0, SCENES)
+    def _(t):
+        k = 8 * (s % 4) + t
+
+        @pl.when(jnp.logical_not(jnp.logical_and(owner == dp, k == s)))
+        def _():
+            hello((owner, k))
+
+    keeps = 4 * dp + s // 8 == s
+    total = HALF + SCENES - 1 + NB - 1 + SCENES
+    pl.semaphore_wait(barrier, total - jnp.where(alone, 1, 0) - jnp.where(keeps, 1, 0))
+
+
 def gather_kernel(
-    od_ref, dkv_ref, w_ref,
-    o_ref, dq_ref, dk_ref, dv_ref, at_ref,
-    ret_a, ret_b, sib, send_b,
-    a_ss, a_rs, b_ss, b_rs, s_ss, s_rs,
+    od_ref, dkv_ref, w_ref, cot_ref,
+    o_ref, dq_ref, dk_ref, dv_ref, wg_ref,
+    ret_a, ret_b, sib, send_b, tiles, group, flat, send_w, recv_w, mine_w, stage,
+    a_ss, a_rs, b_ss, b_rs, s_ss, s_rs, g_ss, g_rs, w_ss, w_rs, f_ss, f_rs,
 ):
     x, c, s = place()
+    dp = x * 2 + c
     alone = c == s % 2
     mine = s // 2
     sibling = (x * 2 + 1 - c, s)
-    greet(x, c, s)
+    greet_all(x, c, s)
 
     def is_self(j):
         return jnp.logical_and(alone, j == mine)
@@ -280,6 +319,21 @@
             src_ref=dkv_ref.at[1 - c, pl.ds(r * 4, 4)], dst_ref=sib.at[pl.ds(r * 4, 4)],
             send_sem=s_ss.at[r], recv_sem=s_rs.at[r],
             device_id=sibling, device_id_type=MESH)
+
+    def g_copy(p, slot):
+        return pltpu.make_async_remote_copy(
+            src_ref=tiles.at[p], dst_ref=group.at[slot], send_sem=g_ss.at[p], recv_sem=g_rs.at[slot],
+            device_id=(p, s), device_id_type=MESH)
+
+    def w_copy(k, slot):
+        return pltpu.make_async_remote_copy(
+            src_ref=send_w.at[k], dst_ref=recv_w.at[slot], send_sem=w_ss.at[k], recv_sem=w_rs.at[slot],
+            device_id=(dp, k), device_id_type=MESH)
+
+    def f_copy(p, slot):
+        return pltpu.make_async_remote_copy(
+            src_ref=mine_w, dst_ref=stage.at[slot], send_sem=f_ss.at[p], recv_sem=f_rs.at[slot],
+            device_id=(p, 4 * dp + s // 8), device_id_type=MESH)
 
     @pl.loop(0, 4)
     def _(t):
@@ -314,6 +368,78 @@
             @pl.when(is_self(j))
             def _():
                 ret_b[mine] = send_b[j]
+
+    @pl.loop(0, HEADS // 2)
+    def _(t):
+        pair = (t + s // 4) % (HEADS // 2)
+        cols = pl.ds(pl.multiple_of(pair * 128, 128), 128)
+        for e in range(2):
+            @pl.when(jnp.logical_not(is_self(pair * 2 + e)))
+            def _():
+                a_copy(pair * 2 + e, pair * 2 + e).wait_recv()
+
+        a0 = ret_a[pair * 2]
+        a1 = ret_a[pair * 2 + 1]
+        at = jnp.concatenate([a0[:, 64:], a1[:, 64:]], axis=1)
+        tiles[pair] = at
+
+        @pl.when(pair != dp)
+        def _():
+            g_copy(pair, dp).start()
+
+        @pl.when(pair == dp)
+        def _():
+            group[dp] = at
+
+        dq_ref[:, cols] = jnp.concatenate([a0[:, 0:64], a1[:, 0:64]], axis=1)
+        flat[:, cols] = at
+
+    @pl.loop(0, SCENES)
+    def _(p):
+        @pl.when(p != dp)
+        def _():
+            g_copy(p, p).wait_recv()
+
+    att = jnp.concatenate([group[p].T for p in range(SCENES)], axis=1)
+    for q in range(4):
+        part = jnp.dot(att, cot_ref[:, q * 256:(q + 1) * 256], preferred_element_type=F32).astype(BF)
+        for r in range(8):
+            send_w[r * 4 + q] = part[r * 16:(r + 1) * 16]
+
+    @pl.loop(1, NB)
+    def _(t):
+        w_copy((s + t) % NB, s).start()
+
+    recv_w[s] = send_w[s]
+
+    @pl.loop(0, 4)
+    def _(t):
+        cols = pl.ds(pl.multiple_of(t * 256, 256), 256)
+        o_ref[:, cols] = jnp.dot(flat[...], w_ref[:, cols], preferred_element_type=F32).astype(BF)
+
+    @pl.loop(1, NB)
+    def _(t):
+        k = (s + NB - t) % NB
+        w_copy(k, k).wait_recv()
+
+    whole = recv_w[0].astype(F32)
+    for k in range(1, NB):
+        whole = whole + recv_w[k].astype(F32)
+    mine_w[...] = whole * (SCENES * NB * BLK) ** (-0.5)
+    keeps = 4 * dp + s // 8 == s
+
+    @pl.loop(0, SCENES)
+    def _(t):
+        p = (dp + t) % SCENES
+        local_end = jnp.logical_and(t == 0, keeps)
+
+        @pl.when(jnp.logical_not(local_end))
+        def _():
+            f_copy(p, s % 8).start()
+
+        @pl.when(local_end)
+        def _():
+            stage[s % 8] = mine_w[...]
 
     @pl.loop(0, HEADS // 2)
     def _(pair):
@@ -321,24 +447,6 @@
         for e in range(2):
             @pl.when(jnp.logical_not(is_self(pair * 2 + e)))
             def _():
-                a_copy(pair * 2 + e, pair * 2 + e).wait_recv()
-
-        a0 = ret_a[pair * 2]
-        a1 = ret_a[pair * 2 + 1]
-        dq_ref[:, cols] = jnp.concatenate([a0[:, 0:64], a1[:, 0:64]], axis=1)
-        at_ref[:, cols] = jnp.concatenate([a0[:, 64:], a1[:, 64:]], axis=1)
-
-    @pl.loop(0, 4)
-    def _(t):
-        cols = pl.ds(pl.multiple_of(t * 256, 256), 256)
-        o_ref[:, cols] = jnp.dot(at_ref[...], w_ref[:, cols], preferred_element_type=F32).astype(BF)
-
-    @pl.loop(0, HEADS // 2)
-    def _(pair):
-        cols = pl.ds(pl.multiple_of(pair * 128, 128), 128)
-        for e in range(2):
-            @pl.when(jnp.logical_not(is_self(pair * 2 + e)))
-            def _():
                 b_copy(pair * 2 + e, pair * 2 + e).wait_recv()
 
         a0 = ret_b[pair * 2]
@@ -346,6 +454,15 @@
         dk_ref[:, cols] = jnp.concatenate([a0[:, 0:64], a1[:, 0:64]], axis=1)
         dv_ref[:, cols] = jnp.concatenate([a0[:, 64:], a1[:, 64:]], axis=1)
 
+    @pl.loop(0, SCENES)
+    def _(t):
+        @pl.when(jnp.logical_not(jnp.logical_and(s // 4 == dp, 8 * (s % 4) + t == s)))
+        def _():
+            f_copy(dp, t).wait_recv()
+
+    for t in range(SCENES):
+        wg_ref[16 * (t // 4):16 * (t // 4) + 16, 256 * (t % 4):256 * (t % 4) + 256] = stage[t]
+
     @pl.loop(0, HALF)
     def _(j):
         @pl.when(jnp.logical_not(is_self(j)))
@@ -356,6 +473,22 @@
     @pl.loop(0, 4)
     def _(r):
         s_copy(r).wait_send()
+
+    @pl.loop(0, SCENES)
+    def _(t):
+        p = (dp + t) % SCENES
+
+        @pl.when(t != 0)
+        def _():
+            g_copy(p, dp).wait_send()
+
+        @pl.when(jnp.logical_not(jnp.logical_and(t == 0, keeps)))
+        def _():
+            f_copy(p, s % 8).wait_send()
+
+    @pl.loop(1, NB)
+    def _(t):
+        w_copy((s + t) % NB, s).wait_send()
 
 
 def spec(n):
@@ -381,6 +514,7 @@
 
 
 def local(node_queries, node_keys, node_values, cotangent, w_out, neighbours, contacts, ownership):
+    cot_all = lax.all_gather(cotangent[0], "dp", axis=0, tiled=True)
     tile = lambda n, t: jax.ShapeDtypeStruct((n, BLK, BLK), t)
     flat = jax.ShapeDtypeStruct((BLK, HEADS * HDIM), BF)
     dma = pltpu.SemaphoreType.DMA
@@ -403,29 +537,22 @@
     parity = (lax.axis_index("dp") % 2).astype(jnp.int32).reshape(1)
     od, dkv = attend(tab, kv, qd, parity)
 
-    output, dq, dk, dv, att = pl.pallas_call(
+    output, dq, dk, dv, weight_grad = pl.pallas_call(
         gather_kernel,
-        out_shape=(flat,) * 5,
-        in_specs=spec(3),
+        out_shape=(flat,) * 4 + (jax.ShapeDtypeStruct((NB, HEADS * HDIM), F32),),
+        in_specs=spec(4),
         out_specs=tuple(spec(5)),
         scratch_shapes=[
             VMEM((HALF, BLK, BLK), BF), VMEM((HALF, BLK, BLK), BF), VMEM((HALF, BLK, BLK), BF), VMEM((HALF, BLK, BLK), BF),
+            VMEM((SCENES, BLK, BLK), BF), VMEM((SCENES, BLK, BLK), BF), VMEM((BLK, HEADS * HDIM), BF),
+            VMEM((NB, 16, 256), BF), VMEM((NB, 16, 256), BF), VMEM((16, 256), F32), VMEM((SCENES, 16, 256), F32),
             dma((HALF,)), dma((HALF,)), dma((HALF,)), dma((HALF,)), dma((4,)), dma((4,)),
+            dma((SCENES,)), dma((SCENES,)), dma((NB,)), dma((NB,)), dma((SCENES,)), dma((SCENES,)),
         ],
         compiler_params=pltpu.CompilerParams(
             collective_id=1, has_side_effects=True, vmem_limit_bytes=32 * 2**20),
         name="gather_nodes",
-    )(od, dkv, w_out)
-
-    scenes = lax.axis_size("dp")
-    cot_all = lax.all_gather(cotangent[0], "dp", axis=0, tiled=True)
-    share = att.reshape(BLK, NB, scenes, NB // scenes)
-    share = lax.all_to_all(share, "dp", split_axis=2, concat_axis=0, tiled=True)
-    share = share.reshape(scenes * BLK, NB * (NB // scenes))
-    part = lax.dot_general(share, cot_all, (((0,), (0,)), ((), ())), preferred_element_type=F32)
-    part = lax.psum_scatter(part.reshape(NB, (NB // scenes) * 1024), "seq", scatter_dimension=0, tiled=True)
-    weight_grad = lax.all_gather(part.reshape(NB // scenes, 1024), "dp", axis=0, tiled=True)
-    weight_grad = weight_grad * (scenes * NB * BLK) ** (-0.5)
+    )(od, dkv, w_out, cot_all)
     return (output[None], dq[None], dk[None], dv[None], weight_grad)
 
 

time: 302 us -> 149 us (0.49); the launches traced: 299 us -> 149 us
  waiting for transfers between devices: 142 us -> 0.68 us
  blocking collectives: 29.9 us -> 0 us
  Pallas kernels: 95.6 us -> 119 us
    unnamed x3 -> x1, waiting for transfers between devices: 142 us -> 0.68 us
    pallas_call x1, Pallas kernels: 30 us -> 53.9 us  [local(): pl.pallas_call(gather_kernel, out_shape=(flat,) * 4 + (jax.ShapeDtypeStru...]
    all_gather x1 -> x0, blocking collectives: 17.9 us -> none  [local(): lax.all_gather(part.reshape(NB // scenes, 1024), 'dp', axis=0, tiled=True)]
    all_to_all x1 -> x0, blocking collectives: 12 us -> none  [local(): share = lax.all_to_all(share, 'dp', split_axis=2, concat_axis=0, tiled=True)]
    unnamed x22 -> x24, local copies, waits for them, and re-layouts: 11.2 us -> 13 us
  transfers between devices with their start and end apart: 2 -> 1, of which waited for: 1 -> 0; matrix products, arithmetic and copies ran while one was open for 1% -> 2% of each run, Pallas kernels for 32% -> 44%
where the time goes in v2:
time: 149 us
  Pallas kernels  119 us (80%)
  local copies, waits for them, and re-layouts  14.5 us (10%)
  between operations  14.1 us (9%)
    pallas_call x1, Pallas kernels, local(): pl.pallas_call(gather_kernel, out_shape=(flat,) * 4 + (jax.ShapeDtypeStru...  53.9 us
    pallas_call x1, Pallas kernels, local(): pl.pallas_call(scatter_kernel, out_shape=(tile(NB, BF), tile(HALF, BF), j...  33.6 us
    pallas_call x1, Pallas kernels, attend(): pl.pallas_call(core_kernel, out_shape=(tile(HALF, BF), jax.ShapeDtypeStru...  31.9 us
    unnamed x24, local copies, waits for them, and re-layouts  13 us
  transfers between devices with their start and end apart: 1, of which 0 were waited for; matrix products, arithmetic and copies ran while one was open for 2% of the time, Pallas kernels for 44%

profile of v2, /device:TPU:17, one launch (start us, length us, event | category | flops | bytes accessed | tf_op | source)
XLA Modules:
  0.0 148.9 jit_solution(16131660616852182717)
XLA Ops:
  7.2 0.0 all-gather.3.cloned.1.call-start
  7.2 0.7 all-gather.3.cloned.1.call-update
  7.9 0.8 copy.13
  8.7 0.8 copy.14
  9.4 0.7 copy.15
  10.2 0.1 pad_add_fusion
  10.3 0.0 copy-start
  10.3 1.6 %copy-done = bf16[1024,1024]{1,0:T(8,128)(2,1)S(1)} copy-done((bf16[1024,1024]{1,0:T(8,128)(2,1)S(1)}, bf16[1024,1024]{1,0:T(8,128)(2,1)}, u32[]{:S(2)}) %copy-start) | copy-done | bytes 2097176
  11.9 0.0 copy-start.3
  11.9 0.9 copy-done.3
  12.8 0.0 copy-start.6
  12.8 0.9 copy-done.6
  13.8 0.0 copy-start.7
  13.8 0.9 copy-done.7
  14.7 0.0 copy-start.8
  14.7 0.9 copy-done.8
  15.7 0.0 copy-start.1
  15.7 33.6 %scatter_heads.1 = (bf16[32,128,128]{2,1,0:T(8,128)(2,1)S(1)}, bf16[16,128,128]{2,1,0:T(8,128)(2,1)S(1)}, s32[32,128]{1,0:T(8,128)S(1)}) custom-call(bf16[128,1024]{1,0:T(8,128)(2,1)S(1)} %bitcast.15, bf16[128,1024]{1,0:T(8,128)(2,1)S(1)} %bitcast.16, bf16[128,1024]{1,0:T(8,128)(2,1)S(1)} %bitcast.17, bf16[128,1024]{1,0:T(8,128)(2,1)S(1)} %bitcast.14, ...), custom_call_target="tpu_custom_call" | custom-call | tf_op jit(solution)/shard_map/scatter_heads/pallas_call | solution.py:523
  49.3 31.9 %attend.1 = (bf16[16,128,128]{2,1,0:T(8,128)(2,1)S(1)}, bf16[2,16,128,128]{3,2,1,0:T(8,128)(2,1)S(1)}) custom-call(s32[32,128]{1,0:T(8,128)S(1)} %get-tuple-element.15.tab_ref, bf16[32,128,128]{2,1,0:T(8,128)(2,1)S(1)} %get-tuple-element.16.kv_ref, bf16[16,128,128]{2,1,0:T(8,128)(2,1)S(1)} %get-tuple-element.17.qd_ref, s32[1]{0:T(128)} %bitcast.7.par_ref), custom_call_target="tpu_custom_call" | custom-call | tf_op jit(solution)/shard_map/attend/pallas_call | solution.py:500
  81.2 0.0 copy-start.4
  81.2 0.8 copy-done.4
  82.0 0.0 all-gather.3.cloned.1.call-done
  82.0 0.0 copy-done.1
  82.0 0.0 copy-start.2
  82.0 1.6 %copy-done.2 = bf16[1,1024,1024]{2,1,0:T(8,128)(2,1)S(1)} copy-done((bf16[1,1024,1024]{2,1,0:T(8,128)(2,1)S(1)}, bf16[1,1024,1024]{2,1,0:T(8,128)(2,1)}, u32[]{:S(2)}) %copy-start.2) | copy-done | bytes 2097176
  83.6 0.0 copy-start.5
  83.6 1.0 copy-done.5
  84.7 53.9 %gather_nodes.1 = (bf16[128,1024]{1,0:T(8,128)(2,1)S(1)}, bf16[128,1024]{1,0:T(8,128)(2,1)S(1)}, bf16[128,1024]{1,0:T(8,128)(2,1)S(1)}, bf16[128,1024]{1,0:T(8,128)(2,1)S(1)}, f32[32,1024]{1,0:T(8,128)S(1)}) custom-call(bf16[16,128,128]{2,1,0:T(8,128)(2,1)S(1)} %copy-done.5, bf16[2,16,128,128]{3,2,1,0:T(8,128)(2,1)S(1)} %get-tuple-element.19.dkv_ref, ...), custom_call_target="tpu_custom_call" | custom-call | tf_op jit(solution)/shard_map/gather_nodes/pallas_call | solution.py:540
  138.6 0.7 copy.21
  139.3 0.7 copy.22
  140.0 0.7 copy.23
  140.7 0.7 copy.24
  141.4 0.7 copy.25
  (1 shorter events, 0.0 us)
Async XLA Ops:
  7.2 74.9 %all-gather.3.cloned.1.call-start = ((), (), s32[]{:S(2)}) async-start(), calls=%async_computation | async-start | bytes 2359296 | tf_op jit(solution)/shard_map/all_gather | solution.py:517
  10.3 1.6 %copy-start = (bf16[1024,1024]{1,0:T(8,128)(2,1)S(1)}, bf16[1024,1024]{1,0:T(8,128)(2,1)}, u32[]{:S(2)}) copy-start(bf16[1024,1024]{1,0:T(8,128)(2,1)} %w_ref.3) | copy-start | bytes 6291460
  11.9 0.9 copy-start.3
  12.8 0.9 copy-start.6
  13.8 0.9 copy-start.7
  14.7 0.9 copy-start.8
  15.7 66.4 %copy-start.1 = (bf16[1024,1024]{1,0:T(8,128)(2,1)S(1)}, bf16[1024,1024]{1,0:T(8,128)(2,1)}, u32[]{:S(2)}) copy-start(bf16[1024,1024]{1,0:T(8,128)(2,1)} %w_ref.3) | copy-start | bytes 6291460
  81.2 0.8 copy-start.4
  82.0 1.6 %copy-start.2 = (bf16[1,1024,1024]{2,1,0:T(8,128)(2,1)S(1)}, bf16[1,1024,1024]{2,1,0:T(8,128)(2,1)}, u32[]{:S(2)}) copy-start(bf16[1,1024,1024]{2,1,0:T(8,128)(2,1)} %all-gather.3.cloned.1.call-done) | copy-start | bytes 6291460
  83.6 1.0 copy-start.5
Sparse Core Ops, SparseCore 0:
  9.9 30.8 all-gather.2

commit v3 on v1

v3 whole, which is shorter than its diff:
```python
import functools

import jax
import jax.numpy as jnp
from jax import lax
from jax.experimental import pallas as pl
from jax.experimental.pallas import tpu as pltpu
from jax.sharding import PartitionSpec as P

HEADS = 16
HDIM = 64
BLK = 128
NB = 32
SCENES = 8
HALF = 16
SLOTS = 13
TILES = HALF * SLOTS
DIM = HEADS * HDIM
MESH = pl.DeviceIdType.MESH
VMEM = pltpu.VMEM
BF = jnp.bfloat16
F32 = jnp.float32


def place():
    dp = lax.axis_index("dp")
    s = lax.axis_index("seq")
    return dp // 2, dp % 2, s


def partner(x, c, s, j):
    return (x * 2 + s % 2, 2 * j + c)


def greet_all(x, c, s):
    barrier = pltpu.get_barrier_semaphore()
    alone = c == s % 2
    dp = x * 2 + c

    def hello(device):
        pl.semaphore_signal(barrier, inc=1, device_id=device, device_id_type=MESH)

    @pl.loop(0, HALF)
    def _(j):
        @pl.when(jnp.logical_not(jnp.logical_and(alone, j == s // 2)))
        def _():
            hello(partner(x, c, s, j))

    @pl.loop(1, SCENES)
    def _(t):
        hello(((dp + t) % SCENES, s))

    y, z = s // 8, s % 8

    @pl.loop(1, 4)
    def _(t):
        hello((dp, (y + t) % 4 * 8 + z))

    @pl.loop(1, 8)
    def _(t):
        hello((dp, y * 8 + (z + t) % 8))

    owner = s // 4

    @pl.loop(0, SCENES)
    def _(t):
        k = 8 * (s % 4) + t

        @pl.when(jnp.logical_not(jnp.logical_and(owner == dp, k == s)))
        def _():
            hello((owner, k))

    keeps = 4 * dp + s // 8 == s
    total = HALF + SCENES - 1 + 3 + 7 + SCENES
    pl.semaphore_wait(barrier, total - jnp.where(alone, 1, 0) - jnp.where(keeps, 1, 0))


def fused_kernel(
    q_hbm, k_hbm, v_hbm, cot_hbm, w_hbm, near_ref, touch_ref, own_ref,
    o_ref, dq_ref, dk_ref, dv_ref, wg_ref,
    q_ref, k_ref, v_ref, w_ref, cot_ref,
    send_kv, send_qd, kv_ref, kvt_ref, qd_ref,
    lists, lists_sib, table, table_s,
    sbuf, pbuf, qd2, qd2t, parts, od_ref, sib_out,
    ret_a, ret_b, sib, send_b, tiles, group, flat, send_y, recv_y, send_z, recv_z, mine_w, stage,
    in_s, kv_ss, kv_rs, qd_ss, qd_rs, re_ss, re_rs, tb_ss, tb_rs, ts_s, cx_ss, cx_rs, cc_ss, cc_rs,
    a_ss, a_rs, b_ss, b_rs, s_ss, s_rs, g_ss, g_rs, y_ss, y_rs, z_ss, z_rs, f_ss, f_rs,
):
    x, c, s = place()
    dp = x * 2 + c
    y, z = s // 8, s % 8
    alone = c == s % 2
    mine = s // 2
    sibling = (x * 2 + 1 - c, s)

    loads = [
        pltpu.make_async_copy(src, dst, in_s.at[n])
        for n, (src, dst) in enumerate(
            ((k_hbm, k_ref), (v_hbm, v_ref), (cot_hbm, cot_ref.at[dp]), (w_hbm, w_ref), (q_hbm, q_ref)))
    ]
    for load in loads:
        load.start()

    def is_self(j):
        return jnp.logical_and(alone, j == mine)

    def remote(src, dst, send, recv, device):
        return pltpu.make_async_remote_copy(
            src_ref=src, dst_ref=dst, send_sem=send, recv_sem=recv, device_id=device, device_id_type=MESH)

    def kv_copy(j, block, slot):
        return remote(send_kv.at[j], kv_ref.at[block], kv_ss.at[j], kv_rs.at[slot], partner(x, c, s, j))

    def qd_copy(j, slot):
        return remote(send_qd.at[j], qd_ref.at[slot], qd_ss.at[j], qd_rs.at[slot], partner(x, c, s, j))

    def relay(j, odd):
        return remote(kv_ref.at[2 * j + odd], kv_ref.at[2 * j + odd], re_ss.at[j], re_rs.at[j], sibling)

    def cot_across(other, source):
        return remote(cot_ref.at[source * 2 + c], cot_ref.at[source * 2 + c], cx_ss.at[other], cx_rs.at[source],
                      (other * 2 + c, s))

    def cot_beside(source, core):
        return remote(cot_ref.at[source * 2 + core], cot_ref.at[source * 2 + core], cc_ss.at[source], cc_rs.at[source],
                      sibling)

    def a_copy(j, slot):
        return remote(od_ref.at[j], ret_a.at[slot], a_ss.at[j], a_rs.at[slot], partner(x, c, s, j))

    def b_copy(j, slot):
        return remote(send_b.at[j], ret_b.at[slot], b_ss.at[j], b_rs.at[slot], partner(x, c, s, j))

    def s_copy(r):
        return remote(sib_out.at[pl.ds(r * 4, 4)], sib.at[pl.ds(r * 4, 4)], s_ss.at[r], s_rs.at[r], sibling)

    def g_copy(p, slot):
        return remote(tiles.at[p], group.at[slot], g_ss.at[p], g_rs.at[slot], (p, s))

    def y_copy(k, slot):
        return remote(send_y.at[pl.ds(k * 8, 8)], recv_y.at[slot], y_ss.at[k], y_rs.at[slot], (dp, k * 8 + z))

    def z_copy(k, slot):
        return remote(send_z.at[k], recv_z.at[slot], z_ss.at[k], z_rs.at[slot], (dp, y * 8 + k))

    def f_copy(p, slot):
        return remote(mine_w, stage.at[slot], f_ss.at[p], f_rs.at[slot], (p, 4 * dp + s // 8))

    lists[...] = jnp.full((BLK, BLK), -1, jnp.int32)
    lists[0:NB, 0:4] = near_ref[...]
    lists[0:NB, 4:12] = touch_ref[...]
    lists[NB:NB + 1, 0:NB] = own_ref[...]
    loads[0].wait()
    loads[1].wait()
    greet_all(x, c, s)
    list_copy = remote(lists, lists_sib, tb_ss, tb_rs, sibling)
    list_copy.start()

    @pl.loop(0, HEADS // 2)
    def _(t):
        pair = (t + s // 4) % (HEADS // 2)
        cols = pl.ds(pl.multiple_of(pair * 128, 128), 128)
        k = k_ref[:, cols]
        v = v_ref[:, cols]
        for e in range(2):
            j = pair * 2 + e
            send_kv[j] = jnp.concatenate([k[:, e * 64:e * 64 + 64], v[:, e * 64:e * 64 + 64]], axis=1)

            @pl.when(jnp.logical_not(is_self(j)))
            def _():
                kv_copy(j, s, mine).start()

            @pl.when(is_self(j))
            def _():
                kv_ref[s] = send_kv[j]

    for load in loads[2:]:
        load.wait()

    @pl.loop(0, HEADS // 2)
    def _(t):
        pair = (t + s // 4) % (HEADS // 2)
        cols = pl.ds(pl.multiple_of(pair * 128, 128), 128)
        q = q_ref[:, cols] * jnp.asarray(0.125, BF)
        d = lax.dot_general(cot_ref[dp], w_ref[cols, :], (((1,), (1,)), ((), ())),
                            preferred_element_type=F32).astype(BF)
        for e in range(2):
            j = pair * 2 + e
            send_qd[j] = jnp.concatenate([q[:, e * 64:e * 64 + 64], d[:, e * 64:e * 64 + 64]], axis=1)

            @pl.when(jnp.logical_not(is_self(j)))
            def _():
                qd_copy(j, mine).start()

            @pl.when(is_self(j))
            def _():
                qd_ref[mine] = send_qd[j]

    cot_beside(x, c).start()

    @pl.loop(1, 4)
    def _(t):
        cot_across((x + t) % 4, x).start()

    list_copy.wait()
    own = jnp.broadcast_to(alone.astype(jnp.int32), (BLK, BLK))
    chosen = lists[...] * own + lists_sib[...] * (1 - own)
    turned = chosen.T
    key_id = lax.broadcasted_iota(jnp.int32, (NB, BLK), 0)
    block_id = lax.broadcasted_iota(jnp.int32, (NB, BLK), 1)
    lane = lax.broadcasted_iota(jnp.int32, (1, BLK), 1)
    first = block_id // 2 * SLOTS
    owner_row = jnp.broadcast_to(chosen[NB:NB + 1, :], (NB, BLK))
    owner_col = jnp.broadcast_to(turned[0:NB, NB:NB + 1], (NB, BLK))
    pos = jnp.where(key_id == block_id, first, TILES)
    table[NB:NB + 1, :] = lane
    table[NB + 16:NB + 17, :] = jnp.ones((1, BLK), jnp.int32)
    for e in range(12):
        entry = turned[e:e + 1, :]
        match = jnp.broadcast_to(entry, (NB, BLK)) == key_id
        if e >= 4:
            match = jnp.logical_and(match, owner_row != owner_col)
        valid = jnp.max(jnp.where(match, 1, 0), axis=0, keepdims=True)
        pos = jnp.where(match, first + (e + 1), pos)
        table[NB + 1 + e:NB + 2 + e, :] = jnp.where(valid > 0, entry, lane)
        table[NB + 17 + e:NB + 18 + e, :] = valid
    table[0:NB, :] = pos
    to_scalar = pltpu.make_async_copy(table, table_s, ts_s)
    to_scalar.start()
    to_scalar.wait()

    qd2[...] = jnp.zeros((2 * BLK, BLK), BF)
    qd2t[...] = jnp.zeros((BLK, 2 * BLK), BF)
    parts[TILES] = jnp.zeros((BLK, BLK), BF)

    @pl.loop(0, HALF)
    def _(t):
        j = (t + mine) % HALF

        @pl.when(jnp.logical_not(is_self(j)))
        def _():
            kv_copy(j, 2 * j + c, j).wait_recv()

        relay(j, c).start()
        kvt_ref[2 * j + c] = kv_ref[2 * j + c].T

    @pl.loop(0, HALF)
    def _(t):
        j = (t + mine) % HALF
        relay(j, 1 - c).wait_recv()
        kvt_ref[2 * j + 1 - c] = kv_ref[2 * j + 1 - c].T

    def fold(part):
        return part.reshape(BLK // 8, 8, BLK)

    spans = [(e, min(2, SLOTS - e)) for e in range(0, SLOTS, 2)]

    @pl.loop(0, HALF)
    def _(t):
        i = 2 * ((mine // 2 - t // 2 + 8) % 8) + t % 2
        b = 2 * i + c

        @pl.when(jnp.logical_not(is_self(i)))
        def _():
            qd_copy(i, i).wait_recv()

        @pl.when(t == 6)
        def _():
            @pl.loop(1, 4)
            def _(u):
                cot_across(x, (x + u) % 4).wait_recv()
                cot_beside((x + u) % 4, c).start()

        slots = [jnp.clip(table_s[NB + e, b], 0, NB - 1) for e in range(SLOTS)]
        qd = qd_ref[i]
        qdt = qd.T
        qd2[0:BLK, 0:HDIM] = qd[:, 0:HDIM]
        qd2[BLK:, HDIM:] = qd[:, HDIM:]
        qd2t[0:HDIM, 0:BLK] = qdt[0:HDIM, :]
        qd2t[HDIM:, BLK:] = qdt[HDIM:, :]

        m = None
        for e, width in spans:
            keys = jnp.concatenate([kv_ref[slots[e + u]] for u in range(width)], axis=0)
            both = jnp.dot(keys, qd2t[...], preferred_element_type=F32)
            for u in range(width):
                part = both[u * BLK:(u + 1) * BLK, 0:BLK]
                if e + u > 0:
                    part = part + (table_s[NB + 16 + e + u, b] - 1).astype(F32) * 1e30
                sbuf[e + u] = part
                pbuf[e + u] = both[u * BLK:(u + 1) * BLK, BLK:]
                top = jnp.max(fold(part), axis=0)
                m = top if m is None else jnp.maximum(m, top)
        m = jnp.broadcast_to(jnp.max(m, axis=0, keepdims=True), (8, BLK))
        total = jnp.zeros((8, BLK), F32)
        dot = jnp.zeros((8, BLK), F32)
        for e in range(SLOTS):
            part = jnp.exp(fold(sbuf[e]) - m[None])
            sbuf[e] = part.reshape(BLK, BLK)
            total = total + jnp.sum(part, axis=0)
            dot = dot + jnp.sum(part * fold(pbuf[e]), axis=0)
        inv = 1.0 / jnp.sum(total, axis=0, keepdims=True)
        delta = jnp.broadcast_to(jnp.sum(dot, axis=0, keepdims=True) * inv, (8, BLK))
        inv = jnp.broadcast_to(inv, (8, BLK))
        mixed = None
        for e, width in spans:
            pieces = []
            for u in range(width):
                prob = fold(sbuf[e + u]) * inv[None]
                ds = prob * (fold(pbuf[e + u]) - delta[None])
                pieces.append(jnp.concatenate(
                    [ds.reshape(BLK, BLK).astype(BF), prob.reshape(BLK, BLK).astype(BF)], axis=1))
            both = jnp.concatenate(pieces, axis=0)
            dkv = jnp.dot(both, qd2[...], preferred_element_type=F32)
            for u in range(width):
                parts[i * SLOTS + e + u] = dkv[u * BLK:(u + 1) * BLK].astype(BF)
            keys = jnp.concatenate([kvt_ref[slots[e + u]] for u in range(width)], axis=1)
            term = jnp.dot(keys, both, preferred_element_type=F32)
            term = (term[0:HDIM, 0:BLK], term[HDIM:, BLK:])
            mixed = term if mixed is None else (mixed[0] + term[0], mixed[1] + term[1])
        od_ref[i] = jnp.concatenate([mixed[0] * 0.125, mixed[1]], axis=0).T.astype(BF)

        @pl.when(jnp.logical_not(is_self(i)))
        def _():
            a_copy(i, mine).start()

        @pl.when(is_self(i))
        def _():
            ret_a[mine] = od_ref[i]

    def gathered(key):
        whole = None
        for i in range(HALF):
            part = parts[jnp.clip(table_s[key, 2 * i + c], 0, TILES)].astype(F32)
            whole = part if whole is None else whole + part
        return whole

    @pl.loop(0, 4)
    def _(t):
        r = (t + s // 8) % 4

        @pl.loop(0, 4)
        def _(u):
            j = r * 4 + u
            sib_out[j] = gathered(2 * j + 1 - c).astype(BF)

        s_copy(r).start()

    def back_chunk(t):
        r = (t + s // 8) % 4
        s_copy(r).wait_recv()

        @pl.loop(0, 4)
        def _(u):
            j = r * 4 + u
            send_b[j] = (gathered(2 * j + c) + sib[j].astype(F32)).astype(BF)

            @pl.when(jnp.logical_not(is_self(j)))
            def _():
                b_copy(j, mine).start()

            @pl.when(is_self(j))
            def _():
                ret_b[mine] = send_b[j]

    @pl.loop(0, HEADS // 2)
    def _(t):
        pair = (t + s // 4) % (HEADS // 2)
        cols = pl.ds(pl.multiple_of(pair * 128, 128), 128)
        for e in range(2):
            @pl.when(jnp.logical_not(is_self(pair * 2 + e)))
            def _():
                a_copy(pair * 2 + e, pair * 2 + e).wait_recv()

        a0 = ret_a[pair * 2]
        a1 = ret_a[pair * 2 + 1]
        at = jnp.concatenate([a0[:, 64:], a1[:, 64:]], axis=1)
        tiles[pair] = at

        @pl.when(pair != dp)
        def _():
            g_copy(pair, dp).start()

        @pl.when(pair == dp)
        def _():
            group[dp] = at

        dq_ref[:, cols] = jnp.concatenate([a0[:, 0:64], a1[:, 0:64]], axis=1)
        flat[:, cols] = at

    @pl.loop(0, 2)
    def _(t):
        back_chunk(t)

    cot_beside(x, 1 - c).wait_recv()

    @pl.loop(1, 4)
    def _(u):
        cot_beside((x + u) % 4, 1 - c).wait_recv()

    @pl.loop(0, SCENES)
    def _(p):
        @pl.when(p != dp)
        def _():
            g_copy(p, p).wait_recv()

    att = jnp.concatenate([group[p].T for p in range(SCENES)], axis=1)
    for q in range(4):
        grads = jnp.concatenate([cot_ref[p, :, q * 256:(q + 1) * 256] for p in range(SCENES)], axis=0)
        part = jnp.dot(att, grads, preferred_element_type=F32).astype(BF)
        for r in range(8):
            send_y[r * 4 + q] = part[r * 16:(r + 1) * 16]

    @pl.loop(1, 4)
    def _(t):
        y_copy((y + t) % 4, y).start()

    recv_y[y] = send_y[pl.ds(y * 8, 8)]

    @pl.loop(2, 4)
    def _(t):
        back_chunk(t)

    @pl.loop(1, 4)
    def _(t):
        k = (y + 4 - t) % 4
        y_copy(k, k).wait_recv()

    for k in range(8):
        send_z[k] = (recv_y[0, k].astype(F32) + recv_y[1, k].astype(F32) + recv_y[2, k].astype(F32)
                     + recv_y[3, k].astype(F32)).astype(BF)

    @pl.loop(1, 8)
    def _(t):
        z_copy((z + t) % 8, z).start()

    recv_z[z] = send_z[z]

    @pl.loop(0, 4)
    def _(t):
        cols = pl.ds(pl.multiple_of(t * 256, 256), 256)
        o_ref[:, cols] = jnp.dot(flat[...], w_ref[:, cols], preferred_element_type=F32).astype(BF)

    @pl.loop(1, 8)
    def _(t):
        k = (z + 8 - t) % 8
        z_copy(k, k).wait_recv()

    whole = recv_z[0].astype(F32)
    for k in range(1, 8):
        whole = whole + recv_z[k].astype(F32)
    mine_w[...] = whole * (SCENES * NB * BLK) ** (-0.5)
    keeps = 4 * dp + s // 8 == s

    @pl.loop(0, SCENES)
    def _(t):
        p = (dp + t) % SCENES
        local_end = jnp.logical_and(t == 0, keeps)

        @pl.when(jnp.logical_not(local_end))
        def _():
            f_copy(p, s % 8).start()

        @pl.when(local_end)
        def _():
            stage[s % 8] = mine_w[...]

    @pl.loop(0, HEADS // 2)
    def _(pair):
        cols = pl.ds(pl.multiple_of(pair * 128, 128), 128)
        for e in range(2):
            @pl.when(jnp.logical_not(is_self(pair * 2 + e)))
            def _():
                b_copy(pair * 2 + e, pair * 2 + e).wait_recv()

        a0 = ret_b[pair * 2]
        a1 = ret_b[pair * 2 + 1]
        dk_ref[:, cols] = jnp.concatenate([a0[:, 0:64], a1[:, 0:64]], axis=1)
        dv_ref[:, cols] = jnp.concatenate([a0[:, 64:], a1[:, 64:]], axis=1)

    @pl.loop(0, SCENES)
    def _(t):
        @pl.when(jnp.logical_not(jnp.logical_and(s // 4 == dp, 8 * (s % 4) + t == s)))
        def _():
            f_copy(dp, t).wait_recv()

    for t in range(SCENES):
        wg_ref[16 * (t // 4):16 * (t // 4) + 16, 256 * (t % 4):256 * (t % 4) + 256] = stage[t]

    @pl.loop(0, HALF)
    def _(j):
        relay(j, c).wait_send()

        @pl.when(jnp.logical_not(is_self(j)))
        def _():
            kv_copy(j, s, mine).wait_send()
            qd_copy(j, mine).wait_send()
            a_copy(j, mine).wait_send()
            b_copy(j, mine).wait_send()

    @pl.loop(0, 4)
    def _(r):
        s_copy(r).wait_send()
        cot_beside(r, c).wait_send()

        @pl.when(r != x)
        def _():
            cot_across(r, x).wait_send()

    @pl.loop(0, SCENES)
    def _(t):
        p = (dp + t) % SCENES

        @pl.when(t != 0)
        def _():
            g_copy(p, dp).wait_send()

        @pl.when(jnp.logical_not(jnp.logical_and(t == 0, keeps)))
        def _():
            f_copy(p, s % 8).wait_send()

    @pl.loop(1, 4)
    def _(t):
        y_copy((y + t) % 4, y).wait_send()

    @pl.loop(1, 8)
    def _(t):
        z_copy((z + t) % 8, z).wait_send()


def local(node_queries, node_keys, node_values, cotangent, w_out, neighbours, contacts, ownership):
    flat = jax.ShapeDtypeStruct((BLK, DIM), BF)
    dma = pltpu.SemaphoreType.DMA
    rows = VMEM((BLK, DIM), BF)
    wide = lambda n, t=BF: VMEM((n, BLK, BLK), t)
    vmem = pl.BlockSpec(memory_space=VMEM)
    output, dq, dk, dv, weight_grad = pl.pallas_call(
        fused_kernel,
        out_shape=(flat,) * 4 + (jax.ShapeDtypeStruct((NB, DIM), F32),),
        in_specs=[pl.BlockSpec(memory_space=pltpu.HBM)] * 5 + [vmem] * 3,
        out_specs=(vmem,) * 5,
        scratch_shapes=[
            rows, rows, rows, VMEM((DIM, DIM), BF), VMEM((SCENES, BLK, DIM), BF),
            wide(HALF), wide(HALF), wide(NB), wide(NB), wide(HALF),
            VMEM((BLK, BLK), jnp.int32), VMEM((BLK, BLK), jnp.int32), VMEM((64, BLK), jnp.int32), pltpu.SMEM((64, BLK), jnp.int32),
            wide(SLOTS, F32), wide(SLOTS, F32), VMEM((2 * BLK, BLK), BF), VMEM((BLK, 2 * BLK), BF),
            wide(TILES + 1), wide(HALF), wide(HALF),
            wide(HALF), wide(HALF), wide(HALF), wide(HALF), wide(SCENES), wide(SCENES), rows,
            VMEM((NB, 16, 256), BF), VMEM((4, 8, 16, 256), BF), VMEM((8, 16, 256), BF), VMEM((8, 16, 256), BF),
            VMEM((16, 256), F32), VMEM((SCENES, 16, 256), F32),
            dma((5,)), dma((HALF,)), dma((HALF,)), dma((HALF,)), dma((HALF,)), dma((HALF,)), dma((HALF,)), dma, dma, dma,
            dma((4,)), dma((4,)), dma((4,)), dma((4,)),
            dma((HALF,)), dma((HALF,)), dma((HALF,)), dma((HALF,)), dma((4,)), dma((4,)),
            dma((SCENES,)), dma((SCENES,)), dma((4,)), dma((4,)), dma((8,)), dma((8,)), dma((SCENES,)), dma((SCENES,)),
        ],
        compiler_params=pltpu.CompilerParams(
            collective_id=0, has_side_effects=True, vmem_limit_bytes=48 * 2**20),
        name="sublayer",
    )(node_queries[0], node_keys[0], node_values[0], cotangent[0], w_out, neighbours[0], contacts[0], ownership)
    return (output[None], dq[None], dk[None], dv[None], weight_grad)


def solution(mesh):
    placed = (
        P("dp", "seq", None), P("dp", "seq", None), P("dp", "seq", None), P("dp", "seq", None),
        P(), P("dp", None, None), P("dp", None, None), P("dp", None),
    )
    return jax.shard_map(
        local,
        mesh=mesh,
        in_specs=placed,
        out_specs=(
            P("dp", "seq", None), P("dp", "seq", None), P("dp", "seq", None), P("dp", "seq", None),
            P("seq", None),
        ),
        check_vma=False,
    )
```

time: 302 us -> 100 us (0.33)
  waiting for transfers between devices: 142 us -> 0 us
  blocking collectives: 29.9 us -> 0 us
  between operations: 14.2 us -> 0.65 us
  Pallas kernels: 95.6 us -> 88 us
  local copies, waits for them, and re-layouts: 15 us -> 11 us
    unnamed x3 -> x0, waiting for transfers between devices: 142 us -> none
    all_gather x1 -> x0, blocking collectives: 17.9 us -> none  [local(): lax.all_gather(part.reshape(NB // scenes, 1024), 'dp', axis=0, tiled=True)]
    all_to_all x1 -> x0, blocking collectives: 12 us -> none  [local(): share = lax.all_to_all(share, 'dp', split_axis=2, concat_axis=0, tiled=True)]
    pallas_call x3 -> x1, Pallas kernels: 95.6 us -> 88 us  [local(): pl.pallas_call(fused_kernel, out_shape=(flat,) * 4 + (jax.ShapeDtypeStruc...]
    unnamed x22 -> x18, local copies, waits for them, and re-layouts: 11.2 us -> 10.3 us
  transfers between devices with their start and end apart: 2 -> 0, of which waited for: 1 -> 0; matrix products, arithmetic and copies ran while one was open for 1% -> 0% of each run, Pallas kernels for 32% -> 0%
where the time goes in v3:
time: 100 us; the launch traced here: 99.7 us
  Pallas kernels  88 us (88%)
  local copies, waits for them, and re-layouts  11 us (11%)
    pallas_call x1, Pallas kernels, local(): pl.pallas_call(fused_kernel, out_shape=(flat,) * 4 + (jax.ShapeDtypeStruc...  88 us
    unnamed x18, local copies, waits for them, and re-layouts  10.3 us

profile of v3, /device:TPU:17, one launch (start us, length us, event | category | flops | bytes accessed | tf_op | source)
XLA Modules:
  0.0 99.7 jit_solution(4971218926692438260)
XLA Ops:
  0.6 0.8 copy.14.near_ref
  1.4 0.8 copy.13
  2.2 0.0 copy-start
  2.2 1.6 %copy-done = bf16[1024,1024]{1,0:T(8,128)(2,1)S(1)} copy-done((bf16[1024,1024]{1,0:T(8,128)(2,1)S(1)}, bf16[1024,1024]{1,0:T(8,128)(2,1)}, u32[]{:S(2)}) %copy-start) | copy-done | bytes 2097176
  3.7 0.0 copy-start.1
  3.7 0.9 copy-done.1
  4.7 0.0 copy-start.2
  4.7 0.9 copy-done.2
  5.6 0.0 copy-start.3
  5.7 0.9 copy-done.3
  6.6 0.0 copy-start.4
  6.6 0.9 copy-done.4
  7.5 0.0 copy-start.5
  7.6 0.7 copy-done.5
  8.2 88.0 %sublayer.1 = (bf16[128,1024]{1,0:T(8,128)(2,1)S(1)}, bf16[128,1024]{1,0:T(8,128)(2,1)S(1)}, bf16[128,1024]{1,0:T(8,128)(2,1)S(1)}, bf16[128,1024]{1,0:T(8,128)(2,1)S(1)}, f32[32,1024]{1,0:T(8,128)S(1)}) custom-call(bf16[128,1024]{1,0:T(8,128)(2,1)S(1)} %bitcast.14, bf16[128,1024]{1,0:T(8,128)(2,1)S(1)} %bitcast.15, bf16[128,1024]{1,0:T(8,128)(2,1)S(1)} %bitcast.16, ...), custom_call_target="tpu_custom_call" | custom-call | tf_op jit(solution)/shard_map/sublayer/pallas_call | solution.py:537
  96.3 0.7 copy.20
  97.0 0.7 copy.21
  97.7 0.7 copy.22
  98.4 0.7 copy.23
  99.1 0.7 copy.24
Async XLA Ops:
  2.2 1.6 %copy-start = (bf16[1024,1024]{1,0:T(8,128)(2,1)S(1)}, bf16[1024,1024]{1,0:T(8,128)(2,1)}, u32[]{:S(2)}) copy-start(bf16[1024,1024]{1,0:T(8,128)(2,1)} %w_hbm.1) | copy-start | bytes 6291460
  3.7 0.9 copy-start.1
  4.7 0.9 copy-start.2
  5.6 0.9 copy-start.3
  6.6 0.9 copy-start.4
  7.5 0.7 copy-start.5

commit v4 on v3

--- a/solution.py
+++ b/solution.py
@@ -229,8 +229,8 @@
     to_scalar.start()
     to_scalar.wait()
 
-    qd2[...] = jnp.zeros((2 * BLK, BLK), BF)
-    qd2t[...] = jnp.zeros((BLK, 2 * BLK), BF)
+    qd2[...] = jnp.zeros((2, 2 * BLK, BLK), BF)
+    qd2t[...] = jnp.zeros((2, BLK, 2 * BLK), BF)
     parts[TILES] = jnp.zeros((BLK, BLK), BF)
 
     @pl.loop(0, HALF)
@@ -255,50 +255,38 @@
 
     spans = [(e, min(2, SLOTS - e)) for e in range(0, SLOTS, 2)]
 
-    @pl.loop(0, HALF)
-    def _(t):
-        i = 2 * ((mine // 2 - t // 2 + 8) % 8) + t % 2
+    def attend(i, k):
         b = 2 * i + c
-
-        @pl.when(jnp.logical_not(is_self(i)))
-        def _():
-            qd_copy(i, i).wait_recv()
-
-        @pl.when(t == 6)
-        def _():
-            @pl.loop(1, 4)
-            def _(u):
-                cot_across(x, (x + u) % 4).wait_recv()
-                cot_beside((x + u) % 4, c).start()
-
         slots = [jnp.clip(table_s[NB + e, b], 0, NB - 1) for e in range(SLOTS)]
         qd = qd_ref[i]
         qdt = qd.T
-        qd2[0:BLK, 0:HDIM] = qd[:, 0:HDIM]
-        qd2[BLK:, HDIM:] = qd[:, HDIM:]
-        qd2t[0:HDIM, 0:BLK] = qdt[0:HDIM, :]
-        qd2t[HDIM:, BLK:] = qdt[HDIM:, :]
-
+        qd2[k, 0:BLK, 0:HDIM] = qd[:, 0:HDIM]
+        qd2[k, BLK:, HDIM:] = qd[:, HDIM:]
+        qd2t[k, 0:HDIM, 0:BLK] = qdt[0:HDIM, :]
+        qd2t[k, HDIM:, BLK:] = qdt[HDIM:, :]
+        yield True
         m = None
         for e, width in spans:
             keys = jnp.concatenate([kv_ref[slots[e + u]] for u in range(width)], axis=0)
-            both = jnp.dot(keys, qd2t[...], preferred_element_type=F32)
+            both = jnp.dot(keys, qd2t[k], preferred_element_type=F32)
             for u in range(width):
                 part = both[u * BLK:(u + 1) * BLK, 0:BLK]
                 if e + u > 0:
                     part = part + (table_s[NB + 16 + e + u, b] - 1).astype(F32) * 1e30
-                sbuf[e + u] = part
-                pbuf[e + u] = both[u * BLK:(u + 1) * BLK, BLK:]
+                sbuf[k * SLOTS + e + u] = part
+                pbuf[k * SLOTS + e + u] = both[u * BLK:(u + 1) * BLK, BLK:]
                 top = jnp.max(fold(part), axis=0)
                 m = top if m is None else jnp.maximum(m, top)
         m = jnp.broadcast_to(jnp.max(m, axis=0, keepdims=True), (8, BLK))
+        yield True
         total = jnp.zeros((8, BLK), F32)
         dot = jnp.zeros((8, BLK), F32)
         for e in range(SLOTS):
-            part = jnp.exp(fold(sbuf[e]) - m[None])
-            sbuf[e] = part.reshape(BLK, BLK)
+            part = jnp.exp(fold(sbuf[k * SLOTS + e]) - m[None])
+            sbuf[k * SLOTS + e] = part.reshape(BLK, BLK)
             total = total + jnp.sum(part, axis=0)
-            dot = dot + jnp.sum(part * fold(pbuf[e]), axis=0)
+            dot = dot + jnp.sum(part * fold(pbuf[k * SLOTS + e]), axis=0)
+        yield True
         inv = 1.0 / jnp.sum(total, axis=0, keepdims=True)
         delta = jnp.broadcast_to(jnp.sum(dot, axis=0, keepdims=True) * inv, (8, BLK))
         inv = jnp.broadcast_to(inv, (8, BLK))
@@ -306,27 +294,49 @@
         for e, width in spans:
             pieces = []
             for u in range(width):
-                prob = fold(sbuf[e + u]) * inv[None]
-                ds = prob * (fold(pbuf[e + u]) - delta[None])
+                prob = fold(sbuf[k * SLOTS + e + u]) * inv[None]
+                ds = prob * (fold(pbuf[k * SLOTS + e + u]) - delta[None])
                 pieces.append(jnp.concatenate(
                     [ds.reshape(BLK, BLK).astype(BF), prob.reshape(BLK, BLK).astype(BF)], axis=1))
             both = jnp.concatenate(pieces, axis=0)
-            dkv = jnp.dot(both, qd2[...], preferred_element_type=F32)
+            dkv = jnp.dot(both, qd2[k], preferred_element_type=F32)
             for u in range(width):
                 parts[i * SLOTS + e + u] = dkv[u * BLK:(u + 1) * BLK].astype(BF)
             keys = jnp.concatenate([kvt_ref[slots[e + u]] for u in range(width)], axis=1)
             term = jnp.dot(keys, both, preferred_element_type=F32)
             term = (term[0:HDIM, 0:BLK], term[HDIM:, BLK:])
             mixed = term if mixed is None else (mixed[0] + term[0], mixed[1] + term[1])
+        yield True
         od_ref[i] = jnp.concatenate([mixed[0] * 0.125, mixed[1]], axis=0).T.astype(BF)
 
-        @pl.when(jnp.logical_not(is_self(i)))
-        def _():
-            a_copy(i, mine).start()
-
-        @pl.when(is_self(i))
-        def _():
-            ret_a[mine] = od_ref[i]
+    @pl.loop(0, HALF // 2)
+    def _(t):
+        i0 = 2 * ((mine // 2 - t + 8) % 8)
+        for k in range(2):
+            @pl.when(jnp.logical_not(is_self(i0 + k)))
+            def _():
+                qd_copy(i0 + k, i0 + k).wait_recv()
+
+        @pl.when(t == 3)
+        def _():
+            @pl.loop(1, 4)
+            def _(u):
+                cot_across(x, (x + u) % 4).wait_recv()
+                cot_beside((x + u) % 4, c).start()
+
+        runs = [attend(i0 + k, k) for k in range(2)]
+        while runs:
+            runs = [run for run in runs if next(run, None)]
+        for k in range(2):
+            i = i0 + k
+
+            @pl.when(jnp.logical_not(is_self(i)))
+            def _():
+                a_copy(i, mine).start()
+
+            @pl.when(is_self(i))
+            def _():
+                ret_a[mine] = od_ref[i]
 
     def gathered(key):
         whole = None
@@ -543,7 +553,7 @@
             rows, rows, rows, VMEM((DIM, DIM), BF), VMEM((SCENES, BLK, DIM), BF),
             wide(HALF), wide(HALF), wide(NB), wide(NB), wide(HALF),
             VMEM((BLK, BLK), jnp.int32), VMEM((BLK, BLK), jnp.int32), VMEM((64, BLK), jnp.int32), pltpu.SMEM((64, BLK), jnp.int32),
-            wide(SLOTS, F32), wide(SLOTS, F32), VMEM((2 * BLK, BLK), BF), VMEM((BLK, 2 * BLK), BF),
+            wide(2 * SLOTS, F32), wide(2 * SLOTS, F32), VMEM((2, 2 * BLK, BLK), BF), VMEM((2, BLK, 2 * BLK), BF),
             wide(TILES + 1), wide(HALF), wide(HALF),
             wide(HALF), wide(HALF), wide(HALF), wide(HALF), wide(SCENES), wide(SCENES), rows,
             VMEM((NB, 16, 256), BF), VMEM((4, 8, 16, 256), BF), VMEM((8, 16, 256), BF), VMEM((8, 16, 256), BF),

time: 100 us -> 93.6 us (0.936)
  Pallas kernels: 88 us -> 81.6 us
    pallas_call x1, Pallas kernels: 88 us -> 81.6 us  [local(): pl.pallas_call(fused_kernel, out_shape=(flat,) * 4 + (jax.ShapeDtypeStruc...]
where the time goes in v4:
time: 93.6 us; the launch traced here: 93.3 us
  Pallas kernels  81.6 us (87%)
  local copies, waits for them, and re-layouts  11 us (12%)
    pallas_call x1, Pallas kernels, local(): pl.pallas_call(fused_kernel, out_shape=(flat,) * 4 + (jax.ShapeDtypeStruc...  81.6 us
    unnamed x18, local copies, waits for them, and re-layouts  10.3 us

profile of v4, /device:TPU:17, one launch (start us, length us, event | category | flops | bytes accessed | tf_op | source)
XLA Modules:
  0.0 93.3 jit_solution(15531807176526447219)
XLA Ops:
  0.6 0.8 copy.14.near_ref
  1.4 0.8 copy.13
  2.2 0.0 copy-start
  2.2 1.6 %copy-done = bf16[1024,1024]{1,0:T(8,128)(2,1)S(1)} copy-done((bf16[1024,1024]{1,0:T(8,128)(2,1)S(1)}, bf16[1024,1024]{1,0:T(8,128)(2,1)}, u32[]{:S(2)}) %copy-start) | copy-done | bytes 2097176
  3.7 0.0 copy-start.1
  3.7 0.9 %copy-done.1 = bf16[1,128,1024]{2,1,0:T(8,128)(2,1)S(1)} copy-done((bf16[1,128,1024]{2,1,0:T(8,128)(2,1)S(1)}, bf16[1,128,1024]{2,1,0:T(8,128)(2,1)}, u32[]{:S(2)}) %copy-start.1) | copy-done | bytes 262168
  4.7 0.0 copy-start.2
  4.7 0.9 %copy-done.2 = bf16[1,128,1024]{2,1,0:T(8,128)(2,1)S(1)} copy-done((bf16[1,128,1024]{2,1,0:T(8,128)(2,1)S(1)}, bf16[1,128,1024]{2,1,0:T(8,128)(2,1)}, u32[]{:S(2)}) %copy-start.2) | copy-done | bytes 262168
  5.6 0.0 copy-start.3
  5.7 0.9 %copy-done.3 = bf16[1,128,1024]{2,1,0:T(8,128)(2,1)S(1)} copy-done((bf16[1,128,1024]{2,1,0:T(8,128)(2,1)S(1)}, bf16[1,128,1024]{2,1,0:T(8,128)(2,1)}, u32[]{:S(2)}) %copy-start.3) | copy-done | bytes 262168
  6.6 0.0 copy-start.4
  6.6 0.9 %copy-done.4 = bf16[1,128,1024]{2,1,0:T(8,128)(2,1)S(1)} copy-done((bf16[1,128,1024]{2,1,0:T(8,128)(2,1)S(1)}, bf16[1,128,1024]{2,1,0:T(8,128)(2,1)}, u32[]{:S(2)}) %copy-start.4) | copy-done | bytes 262168
  7.5 0.0 copy-start.5
  7.6 0.7 copy-done.5
  8.2 81.6 %sublayer.1 = (bf16[128,1024]{1,0:T(8,128)(2,1)S(1)}, bf16[128,1024]{1,0:T(8,128)(2,1)S(1)}, bf16[128,1024]{1,0:T(8,128)(2,1)S(1)}, bf16[128,1024]{1,0:T(8,128)(2,1)S(1)}, f32[32,1024]{1,0:T(8,128)S(1)}) custom-call(bf16[128,1024]{1,0:T(8,128)(2,1)S(1)} %bitcast.14, bf16[128,1024]{1,0:T(8,128)(2,1)S(1)} %bitcast.15, bf16[128,1024]{1,0:T(8,128)(2,1)S(1)} %bitcast.16, ...), custom_call_target="tpu_custom_call" | custom-call | tf_op jit(solution)/shard_map/sublayer/pallas_call | solution.py:547
  89.8 0.7 copy.20
  90.5 0.7 copy.21
  91.2 0.7 copy.22
  91.9 0.7 copy.23
  92.6 0.7 copy.24
Async XLA Ops:
  2.2 1.6 %copy-start = (bf16[1024,1024]{1,0:T(8,128)(2,1)S(1)}, bf16[1024,1024]{1,0:T(8,128)(2,1)}, u32[]{:S(2)}) copy-start(bf16[1024,1024]{1,0:T(8,128)(2,1)} %w_hbm.1) | copy-start | bytes 6291460
  3.7 0.9 %copy-start.1 = (bf16[1,128,1024]{2,1,0:T(8,128)(2,1)S(1)}, bf16[1,128,1024]{2,1,0:T(8,128)(2,1)}, u32[]{:S(2)}) copy-start(bf16[1,128,1024]{2,1,0:T(8,128)(2,1)} %param.8) | copy-start | bytes 786436
  4.7 0.9 %copy-start.2 = (bf16[1,128,1024]{2,1,0:T(8,128)(2,1)S(1)}, bf16[1,128,1024]{2,1,0:T(8,128)(2,1)}, u32[]{:S(2)}) copy-start(bf16[1,128,1024]{2,1,0:T(8,128)(2,1)} %param.9) | copy-start | bytes 786436
  5.6 0.9 %copy-start.3 = (bf16[1,128,1024]{2,1,0:T(8,128)(2,1)S(1)}, bf16[1,128,1024]{2,1,0:T(8,128)(2,1)}, u32[]{:S(2)}) copy-start(bf16[1,128,1024]{2,1,0:T(8,128)(2,1)} %param.10) | copy-start | bytes 786436
  6.6 0.9 %copy-start.4 = (bf16[1,128,1024]{2,1,0:T(8,128)(2,1)S(1)}, bf16[1,128,1024]{2,1,0:T(8,128)(2,1)}, u32[]{:S(2)}) copy-start(bf16[1,128,1024]{2,1,0:T(8,128)(2,1)} %param.11) | copy-start | bytes 786436
  7.5 0.7 copy-start.5

commit v5 on v4

--- a/solution.py
+++ b/solution.py
@@ -70,7 +70,11 @@
         def _():
             hello((owner, k))
 
-    keeps = 4 * dp + s // 8 == s
+
+def await_all(x, c, s):
+    barrier = pltpu.get_barrier_semaphore()
+    alone = c == s % 2
+    keeps = 4 * (x * 2 + c) + s // 8 == s
     total = HALF + SCENES - 1 + 3 + 7 + SCENES
     pl.semaphore_wait(barrier, total - jnp.where(alone, 1, 0) - jnp.where(keeps, 1, 0))
 
@@ -100,6 +104,7 @@
     ]
     for load in loads:
         load.start()
+    greet_all(x, c, s)
 
     def is_self(j):
         return jnp.logical_and(alone, j == mine)
@@ -152,9 +157,6 @@
     lists[NB:NB + 1, 0:NB] = own_ref[...]
     loads[0].wait()
     loads[1].wait()
-    greet_all(x, c, s)
-    list_copy = remote(lists, lists_sib, tb_ss, tb_rs, sibling)
-    list_copy.start()
 
     @pl.loop(0, HEADS // 2)
     def _(t):
@@ -166,13 +168,21 @@
             j = pair * 2 + e
             send_kv[j] = jnp.concatenate([k[:, e * 64:e * 64 + 64], v[:, e * 64:e * 64 + 64]], axis=1)
 
-            @pl.when(jnp.logical_not(is_self(j)))
-            def _():
-                kv_copy(j, s, mine).start()
-
-            @pl.when(is_self(j))
-            def _():
-                kv_ref[s] = send_kv[j]
+    await_all(x, c, s)
+    list_copy = remote(lists, lists_sib, tb_ss, tb_rs, sibling)
+    list_copy.start()
+
+    @pl.loop(0, HALF)
+    def _(t):
+        j = (t + s // 4 * 2) % HALF
+
+        @pl.when(jnp.logical_not(is_self(j)))
+        def _():
+            kv_copy(j, s, mine).start()
+
+        @pl.when(is_self(j))
+        def _():
+            kv_ref[s] = send_kv[j]
 
     for load in loads[2:]:
         load.wait()
@@ -398,9 +408,7 @@
         dq_ref[:, cols] = jnp.concatenate([a0[:, 0:64], a1[:, 0:64]], axis=1)
         flat[:, cols] = at
 
-    @pl.loop(0, 2)
-    def _(t):
-        back_chunk(t)
+    back_chunk(0)
 
     cot_beside(x, 1 - c).wait_recv()
 
@@ -427,9 +435,7 @@
 
     recv_y[y] = send_y[pl.ds(y * 8, 8)]
 
-    @pl.loop(2, 4)
-    def _(t):
-        back_chunk(t)
+    back_chunk(1)
 
     @pl.loop(1, 4)
     def _(t):
@@ -445,6 +451,7 @@
         z_copy((z + t) % 8, z).start()
 
     recv_z[z] = send_z[z]
+    back_chunk(2)
 
     @pl.loop(0, 4)
     def _(t):
@@ -474,6 +481,8 @@
         @pl.when(local_end)
         def _():
             stage[s % 8] = mine_w[...]
+
+    back_chunk(3)
 
     @pl.loop(0, HEADS // 2)
     def _(pair):
@@ -564,7 +573,7 @@
             dma((SCENES,)), dma((SCENES,)), dma((4,)), dma((4,)), dma((8,)), dma((8,)), dma((SCENES,)), dma((SCENES,)),
         ],
         compiler_params=pltpu.CompilerParams(
-            collective_id=0, has_side_effects=True, vmem_limit_bytes=48 * 2**20),
+            collective_id=0, has_side_effects=True, vmem_limit_bytes=53 * 2**20),
         name="sublayer",
     )(node_queries[0], node_keys[0], node_values[0], cotangent[0], w_out, neighbours[0], contacts[0], ownership)
     return (output[None], dq[None], dk[None], dv[None], weight_grad)

time: 93.6 us -> 88.3 us (0.943)
  local copies, waits for them, and re-layouts: 11 us -> 6.61 us
  Pallas kernels: 81.6 us -> 80.3 us
    unnamed x18 -> x8, local copies, waits for them, and re-layouts: 10.3 us -> 5.85 us
    pallas_call x1, Pallas kernels: 81.6 us -> 80.3 us  [local(): pl.pallas_call(fused_kernel, out_shape=(flat,) * 4 + (jax.ShapeDtypeStruc...]
where the time goes in v5:
time: 88.3 us; the launch traced here: 87.5 us
  Pallas kernels  80.3 us (91%)
  local copies, waits for them, and re-layouts  6.61 us (7%)
    pallas_call x1, Pallas kernels, local(): pl.pallas_call(fused_kernel, out_shape=(flat,) * 4 + (jax.ShapeDtypeStruc...  80.3 us
    unnamed x8, local copies, waits for them, and re-layouts  5.85 us

profile of v5, /device:TPU:17, one launch (start us, length us, event | category | flops | bytes accessed | tf_op | source)
XLA Modules:
  0.0 87.5 jit_solution(3409951589425639363)
XLA Ops:
  0.6 0.8 copy.14.near_ref
  1.4 0.8 copy.13
  2.2 0.0 copy-start
  2.2 0.7 copy-done
  2.8 80.3 %sublayer.1 = (bf16[128,1024]{1,0:T(8,128)(2,1)S(1)}, bf16[128,1024]{1,0:T(8,128)(2,1)S(1)}, bf16[128,1024]{1,0:T(8,128)(2,1)S(1)}, bf16[128,1024]{1,0:T(8,128)(2,1)}, f32[32,1024]{1,0:T(8,128)S(1)}) custom-call(bf16[128,1024]{1,0:T(8,128)(2,1)} %bitcast.15, bf16[128,1024]{1,0:T(8,128)(2,1)} %bitcast.16, bf16[128,1024]{1,0:T(8,128)(2,1)} %bitcast.17, ...), custom_call_target="tpu_custom_call" | custom-call | tf_op jit(solution)/shard_map/sublayer/pallas_call | solution.py:556
  83.1 0.7 copy.20
  83.8 0.7 copy.21
  84.5 0.7 copy.22
  85.2 1.7 %copy.23 = bf16[1,128,1024]{2,1,0:T(8,128)(2,1)} copy(bf16[1,128,1024]{2,1,0:T(8,128)(2,1)} %bitcast.14) | data formatting | bytes 524288
  86.9 0.7 copy.24
Async XLA Ops:
  2.2 0.7 copy-start

commit v6 on v5

--- a/solution.py
+++ b/solution.py
@@ -243,22 +243,29 @@
     qd2t[...] = jnp.zeros((2, BLK, 2 * BLK), BF)
     parts[TILES] = jnp.zeros((BLK, BLK), BF)
 
-    @pl.loop(0, HALF)
-    def _(t):
-        j = (t + mine) % HALF
-
-        @pl.when(jnp.logical_not(is_self(j)))
-        def _():
-            kv_copy(j, 2 * j + c, j).wait_recv()
-
-        relay(j, c).start()
-        kvt_ref[2 * j + c] = kv_ref[2 * j + c].T
-
-    @pl.loop(0, HALF)
-    def _(t):
+    def relayed(t):
         j = (t + mine) % HALF
         relay(j, 1 - c).wait_recv()
         kvt_ref[2 * j + 1 - c] = kv_ref[2 * j + 1 - c].T
+
+    @pl.loop(0, HALF)
+    def _(t):
+        j = (t + mine) % HALF
+
+        @pl.when(jnp.logical_not(is_self(j)))
+        def _():
+            kv_copy(j, 2 * j + c, j).wait_recv()
+
+        relay(j, c).start()
+        kvt_ref[2 * j + c] = kv_ref[2 * j + c].T
+
+        @pl.when(t >= 4)
+        def _():
+            relayed(t - 4)
+
+    @pl.loop(HALF - 4, HALF)
+    def _(t):
+        relayed(t)
 
     def fold(part):
         return part.reshape(BLK // 8, 8, BLK)
@@ -383,6 +390,8 @@
             def _():
                 ret_b[mine] = send_b[j]
 
+    back_chunk(0)
+
     @pl.loop(0, HEADS // 2)
     def _(t):
         pair = (t + s // 4) % (HEADS // 2)
@@ -408,7 +417,6 @@
         dq_ref[:, cols] = jnp.concatenate([a0[:, 0:64], a1[:, 0:64]], axis=1)
         flat[:, cols] = at
 
-    back_chunk(0)
 
     cot_beside(x, 1 - c).wait_recv()
 
@@ -573,7 +581,7 @@
             dma((SCENES,)), dma((SCENES,)), dma((4,)), dma((4,)), dma((8,)), dma((8,)), dma((SCENES,)), dma((SCENES,)),
         ],
         compiler_params=pltpu.CompilerParams(
-            collective_id=0, has_side_effects=True, vmem_limit_bytes=53 * 2**20),
+            collective_id=0, has_side_effects=True, vmem_limit_bytes=55259136),
         name="sublayer",
     )(node_queries[0], node_keys[0], node_values[0], cotangent[0], w_out, neighbours[0], contacts[0], ownership)
     return (output[None], dq[None], dk[None], dv[None], weight_grad)

time: 88.3 us -> 88.2 us (level)
  Pallas kernels: 80.3 us -> 81.4 us
  local copies, waits for them, and re-layouts: 6.61 us -> 5.65 us
    pallas_call x1, Pallas kernels: 80.3 us -> 81.4 us  [local(): pl.pallas_call(fused_kernel, out_shape=(flat,) * 4 + (jax.ShapeDtypeStruc...]
    unnamed x8, local copies, waits for them, and re-layouts: 5.85 us -> 4.88 us
where the time goes in v6:
time: 88.2 us; the launch traced here: 87.7 us
  Pallas kernels  81.4 us (92%)
  local copies, waits for them, and re-layouts  5.65 us (6%)
    pallas_call x1, Pallas kernels, local(): pl.pallas_call(fused_kernel, out_shape=(flat,) * 4 + (jax.ShapeDtypeStruc...  81.4 us
    unnamed x8, local copies, waits for them, and re-layouts  4.88 us

profile of v6, /device:TPU:17, one launch (start us, length us, event | category | flops | bytes accessed | tf_op | source)
XLA Modules:
  0.0 87.7 jit_solution(14464540311916452571)
XLA Ops:
  0.6 0.8 copy.14.near_ref
  1.4 0.8 copy.13
  2.2 0.0 copy-start
  2.2 0.7 copy-done
  2.8 81.4 %sublayer.1 = (bf16[128,1024]{1,0:T(8,128)(2,1)S(1)}, bf16[128,1024]{1,0:T(8,128)(2,1)S(1)}, bf16[128,1024]{1,0:T(8,128)(2,1)S(1)}, bf16[128,1024]{1,0:T(8,128)(2,1)S(1)}, f32[32,1024]{1,0:T(8,128)S(1)}) custom-call(bf16[128,1024]{1,0:T(8,128)(2,1)} %bitcast.15, bf16[128,1024]{1,0:T(8,128)(2,1)} %bitcast.16, bf16[128,1024]{1,0:T(8,128)(2,1)} %bitcast.17, ...), custom_call_target="tpu_custom_call" | custom-call | tf_op jit(solution)/shard_map/sublayer/pallas_call | solution.py:564
  84.3 0.7 copy.20
  85.0 0.7 copy.21
  85.7 0.7 copy.22
  86.4 0.7 copy.23
  87.1 0.7 copy.24
Async XLA Ops:
  2.2 0.7 copy-start

commit v7 on v5

--- a/solution.py
+++ b/solution.py
@@ -405,7 +405,6 @@
         def _():
             group[dp] = at
 
-        dq_ref[:, cols] = jnp.concatenate([a0[:, 0:64], a1[:, 0:64]], axis=1)
         flat[:, cols] = at
 
     back_chunk(0)
@@ -457,6 +456,11 @@
     def _(t):
         cols = pl.ds(pl.multiple_of(t * 256, 256), 256)
         o_ref[:, cols] = jnp.dot(flat[...], w_ref[:, cols], preferred_element_type=F32).astype(BF)
+
+    @pl.loop(0, HEADS // 2)
+    def _(pair):
+        cols = pl.ds(pl.multiple_of(pair * 128, 128), 128)
+        dq_ref[:, cols] = jnp.concatenate([ret_a[pair * 2][:, 0:64], ret_a[pair * 2 + 1][:, 0:64]], axis=1)
 
     @pl.loop(1, 8)
     def _(t):
@@ -573,7 +577,7 @@
             dma((SCENES,)), dma((SCENES,)), dma((4,)), dma((4,)), dma((8,)), dma((8,)), dma((SCENES,)), dma((SCENES,)),
         ],
         compiler_params=pltpu.CompilerParams(
-            collective_id=0, has_side_effects=True, vmem_limit_bytes=53 * 2**20),
+            collective_id=0, has_side_effects=True, vmem_limit_bytes=55259136),
         name="sublayer",
     )(node_queries[0], node_keys[0], node_values[0], cotangent[0], w_out, neighbours[0], contacts[0], ownership)
     return (output[None], dq[None], dk[None], dv[None], weight_grad)

time: 88.3 us -> 86.3 us (0.977)
  local copies, waits for them, and re-layouts: 6.61 us -> 5.65 us
    unnamed x8, local copies, waits for them, and re-layouts: 5.85 us -> 4.88 us
where the time goes in v7:
time: 86.3 us; the launch traced here: 86.1 us
  Pallas kernels  79.9 us (93%)
  local copies, waits for them, and re-layouts  5.65 us (7%)
    pallas_call x1, Pallas kernels, local(): pl.pallas_call(fused_kernel, out_shape=(flat,) * 4 + (jax.ShapeDtypeStruc...  79.9 us
    unnamed x8, local copies, waits for them, and re-layouts  4.88 us

profile of v7, /device:TPU:17, one launch (start us, length us, event | category | flops | bytes accessed | tf_op | source)
XLA Modules:
  0.0 86.1 jit_solution(609711614156817534)
XLA Ops:
  0.6 0.8 copy.14.near_ref
  1.4 0.8 copy.13
  2.2 0.0 copy-start
  2.2 0.7 copy-done
  2.8 79.9 %sublayer.1 = (bf16[128,1024]{1,0:T(8,128)(2,1)S(1)}, bf16[128,1024]{1,0:T(8,128)(2,1)S(1)}, bf16[128,1024]{1,0:T(8,128)(2,1)S(1)}, bf16[128,1024]{1,0:T(8,128)(2,1)S(1)}, f32[32,1024]{1,0:T(8,128)S(1)}) custom-call(bf16[128,1024]{1,0:T(8,128)(2,1)} %bitcast.15, bf16[128,1024]{1,0:T(8,128)(2,1)} %bitcast.16, bf16[128,1024]{1,0:T(8,128)(2,1)} %bitcast.17, ...), custom_call_target="tpu_custom_call" | custom-call | tf_op jit(solution)/shard_map/sublayer/pallas_call | solution.py:560
  82.7 0.7 copy.20
  83.4 0.7 copy.21
  84.1 0.7 copy.22
  84.8 0.7 copy.23
  85.5 0.7 copy.24
Async XLA Ops:
  2.2 0.7 copy-start
